TPU v7x, 32 devices: a whole 2x2x4 slice. The times are simulated.
32 devices in a mesh: dp: 4 (over x, core), expert: 8 (over z, y).
Axes of the slice: x: 2, y: 2, z: 4, core: 2. Of those that a mesh axis runs over, the one named last changes fastest.
Arguments:
- tokens: bfloat16 [4096, 5120], P(('dp', 'expert')), may hold values from -6 to 6
- cotangent: bfloat16 [4096, 5120], P(('dp', 'expert')), may hold values from -6 to 6
- gate: float32 [4096], P(('dp', 'expert')), may hold values from 0.25 to 2
- clade: int32 [4096], P(('dp', 'expert')), may hold values from 0 to 7
- block: int32 [4096], P(('dp', 'expert')), may hold values from 0 to 20, as said below
- plan: int32 [8], replicated, may hold values from 0 to 7, as said below
- w_gu: bfloat16 [8, 2, 1408, 5120], P('expert', None, 'dp'), may hold values from -0.078125 to 0.078125
- w_down: bfloat16 [8, 1408, 5120], P('expert', 'dp'), may hold values from -0.15625 to 0.15625
Outputs:
- grad_tokens: bfloat16 [4096, 5120], P(('dp', 'expert'))
- grad_gu: bfloat16 [8, 2, 1408, 5120], P('expert', None, 'dp')
- grad_down: bfloat16 [8, 1408, 5120], P('expert', 'dp')
Inputs may be any that keep to these rules, and one draw needn't show every extreme that they name: plan[e] is e (no replica) or (e + 4) mod 8; experts 0, 3, 4 and 7 always have a replica. A value below 16 places the token in its owner's block, 16 to 19 in its replica's block (only for experts with a replica), 20 drops it; among the 128 tokens of one device, tokens of the same clade have distinct values below 20.
All inputs are finite; a program needn't handle non-finite values.
Results may differ from a plain program's by a relative error of at most 0.0066.
Values may be sent and summed in bfloat16 or wider, within the bound.
A program may use at most 192 MiB of HBM per device.

v0:
```python
import jax
import jax.numpy as jnp
from jax import lax
from jax.sharding import PartitionSpec as P


def partner(value, axis, stride):
    mask = 2**stride
    pairs = [(source, source ^ mask) for source in range(lax.axis_size(axis))]
    return lax.ppermute(value, axis, pairs)


def expert_pass(rows_x, rows_cot, weights):
    contract_last = (((1,), (1,)), ((), ()))
    contract_rows = (((0,), (0,)), ((), ()))
    gate_pre = lax.dot_general(
        rows_x, weights[0], contract_last, preferred_element_type=jnp.float32
    )
    up_pre = lax.dot_general(rows_x, weights[1], contract_last, preferred_element_type=jnp.float32)
    sigmoid = jax.nn.sigmoid(gate_pre)
    hidden = (gate_pre * sigmoid * up_pre).astype(jnp.bfloat16)
    hidden_cot = lax.dot_general(
        rows_cot, weights[2], contract_last, preferred_element_type=jnp.float32
    )
    up_cot = (hidden_cot * gate_pre * sigmoid).astype(jnp.bfloat16)
    gate_cot = (hidden_cot * up_pre * sigmoid * (1.0 + gate_pre * (1.0 - sigmoid))).astype(
        jnp.bfloat16
    )
    grads = jnp.stack(
        [
            lax.dot_general(gate_cot, rows_x, contract_rows, preferred_element_type=jnp.float32),
            lax.dot_general(up_cot, rows_x, contract_rows, preferred_element_type=jnp.float32),
            lax.dot_general(hidden, rows_cot, contract_rows, preferred_element_type=jnp.float32),
        ]
    ).astype(jnp.bfloat16)
    partial_value = jnp.dot(gate_cot, weights[0], preferred_element_type=jnp.float32)
    partial_value = (
        partial_value + jnp.dot(up_cot, weights[1], preferred_element_type=jnp.float32)
    ).astype(jnp.bfloat16)
    return (grads, partial_value)


def local(tokens, cotangent, gate, clade, block, plan, w_gu, w_down):
    columns = lax.axis_size("expert")
    groups = lax.axis_size("dp")
    tok_rows = tokens.shape[0]
    width = tokens.shape[1]
    cap_home = tok_rows // columns
    cap_guest = tok_rows // (4 * columns)
    cap_rows = cap_home + cap_guest
    slot_count = columns * cap_rows
    experts = plan.shape[0]
    matches = clade[:, None] == jnp.arange(experts, dtype=jnp.int32)[None, :]
    lookup = jnp.sum(jnp.where(matches, plan[None, :], 0), axis=1)
    target = jnp.where(block < cap_home, clade, lookup)
    slot = jnp.where(block < cap_rows, target * cap_rows + block, -1)
    selector = (jnp.arange(slot_count, dtype=jnp.int32)[:, None] == slot[None, :]).astype(
        jnp.bfloat16
    )
    scaled = (gate[:, None] * cotangent.astype(jnp.float32)).astype(jnp.bfloat16)
    send_x = jnp.dot(selector, tokens, preferred_element_type=jnp.float32).astype(jnp.bfloat16)
    send_c = jnp.dot(selector, scaled, preferred_element_type=jnp.float32).astype(jnp.bfloat16)
    copies_x = jnp.broadcast_to(send_x[None], (groups, slot_count, width)).reshape(
        groups * slot_count, width
    )
    copies_c = jnp.broadcast_to(send_c[None], (groups, slot_count, width)).reshape(
        groups * slot_count, width
    )
    got_x, got_c = (
        lax.all_to_all(copies_x, ("dp", "expert"), split_axis=0, concat_axis=0, tiled=True),
        lax.all_to_all(copies_c, ("dp", "expert"), split_axis=0, concat_axis=0, tiled=True),
    )
    senders = got_x.shape[0] // cap_rows
    shaped_x = got_x.reshape(senders, cap_rows, width)
    shaped_c = got_c.reshape(senders, cap_rows, width)
    home_x = shaped_x[:, :cap_home].reshape(senders * cap_home, width)
    home_c = shaped_c[:, :cap_home].reshape(senders * cap_home, width)
    guest_x = shaped_x[:, cap_home:].reshape(senders * cap_guest, width)
    guest_c = shaped_c[:, cap_home:].reshape(senders * cap_guest, width)
    own_weights = jnp.concatenate([w_gu[0], w_down], axis=0)
    pair_bit = columns.bit_length() - 2
    home_grads, home_part = expert_pass(home_x, home_c, own_weights)
    guest_weights = partner(own_weights, "expert", pair_bit)
    guest_grads, guest_part = expert_pass(guest_x, guest_c, guest_weights)
    returned = partner(guest_grads, "expert", pair_bit)
    total = (home_grads.astype(jnp.float32) + returned.astype(jnp.float32)).astype(jnp.bfloat16)
    part = jnp.concatenate(
        [
            home_part.reshape(senders, cap_home, width),
            guest_part.reshape(senders, cap_guest, width),
        ],
        axis=1,
    )
    part = part.reshape(senders * cap_rows, width)
    arrived = lax.all_to_all(part, ("dp", "expert"), split_axis=0, concat_axis=0, tiled=True)
    result = jnp.sum(arrived.reshape(groups, slot_count, width).astype(jnp.float32), axis=0).astype(
        jnp.bfloat16
    )
    grad_tokens = lax.dot_general(
        selector, result, (((0,), (0,)), ((), ())), preferred_element_type=jnp.float32
    )
    return (grad_tokens.astype(jnp.bfloat16), total[:2][None], total[2:3])


def solution(mesh):
    placed = (
        P(("dp", "expert"), None),
        P(("dp", "expert"), None),
        P(("dp", "expert")),
        P(("dp", "expert")),
        P(("dp", "expert")),
        P(),
        P("expert", None, "dp", None),
        P("expert", "dp", None),
    )
    return jax.shard_map(
        local,
        mesh=mesh,
        in_specs=placed,
        out_specs=(
            P(("dp", "expert"), None),
            P("expert", None, "dp", None),
            P("expert", "dp", None),
        ),
        check_vma=False,
    )
```

profile of v0, /device:TPU:0, one launch (start us, length us, event | category | flops | bytes accessed | tf_op | source)
XLA Modules:
  0.0 1534.2 jit_solution(2809921882110335785)
XLA Ops:
  2.8 3.6 broadcast_in_dim.41
  6.4 8.5 all_to_all.18
  14.9 7.4 all-to-all-start.1
  23.0 3.6 broadcast_in_dim.40
  26.6 8.5 all_to_all.16
  35.1 165.7 %all-to-all-done.1 = bf16[32,20,5120]{2,1,0:T(8,128)(2,1)} async-done(((bf16[32,20,5120]{2,1,0:T(8,128)(2,1)}), bf16[32,20,5120]{2,1,0:T(8,128)(2,1)}, u32[]{:S(2)}, u32[]{:S(2)}) %all-to-all-start.1) | async-done | bytes 6553632 | tf_op jit(solution)/shard_map/all_to_all | solution.py:70
  200.8 3.7 all-to-all-start
  204.5 10.0 pad_maximum_fusion
  219.5 395.0 %all-to-all-done = bf16[32,20,5120]{2,1,0:T(8,128)(2,1)} async-done(((bf16[32,20,5120]{2,1,0:T(8,128)(2,1)}), bf16[32,20,5120]{2,1,0:T(8,128)(2,1)}, u32[]{:S(2)}, u32[]{:S(2)}) %all-to-all-start) | async-done | bytes 6553632 | tf_op jit(solution)/shard_map/all_to_all | solution.py:71
  617.9 3.0 slice.51
  620.9 6.9 fusion.10
  627.8 2.9 fusion.13
  630.7 210.1 %collective-permute-done = bf16[3,352,5120]{2,1,0:T(8,128)(2,1)} collective-permute-done((bf16[3,352,5120]{2,1,0:T(8,128)(2,1)}, bf16[3,352,5120]{2,1,0:T(8,128)(2,1)}, u32[]{:S(2)}, u32[]{:S(2)}) %collective-permute-start) | collective-permute-done | bytes 10813472 | tf_op jit(solution)/shard_map/ppermute | solution.py:10
  840.8 3.1 fusion.19
  844.0 3.2 fusion.18
  847.2 2.9 fusion.2
  850.1 3.1 multiply_convert_fusion.8
  861.9 2.9 fusion.6
  865.7 3.0 slice.50
  873.6 2.9 fusion.8
  877.8 5.1 pad_maximum_fusion.1
  882.8 5.4 add_convert_fusion.1
  888.3 4.3 pad_maximum_fusion.2
  892.6 9.6 all-to-all-start.2
  902.2 4.7 fusion.4
  906.9 4.6 fusion.3
  913.7 519.4 %collective-permute-done.1 = bf16[3,352,5120]{2,1,0:T(8,128)(2,1)} collective-permute-done((bf16[3,352,5120]{2,1,0:T(8,128)(2,1)}, bf16[3,352,5120]{2,1,0:T(8,128)(2,1)}, u32[]{:S(2)}, u32[]{:S(2)}) %collective-permute-start.1) | collective-permute-done | bytes 10813472 | tf_op jit(solution)/shard_map/ppermute | solution.py:10
  1433.1 8.0 add_convert_fusion
  1443.1 3.5 slice_bitcast_fusion
  1446.6 73.1 %all-to-all-done.2 = bf16[32,20,5120]{2,1,0:T(8,128)(2,1)} async-done(((bf16[32,20,5120]{2,1,0:T(8,128)(2,1)}), bf16[32,20,5120]{2,1,0:T(8,128)(2,1)}, u32[]{:S(2)}, u32[]{:S(2)}) %all-to-all-start.2) | async-done | bytes 6553632 | tf_op jit(solution)/shard_map/all_to_all | solution.py:95
  1519.6 8.7 reshape.60
  1528.4 4.2 reduce_sum.22
  (61 shorter events, 32.5 us)
Async XLA Ops:
  0.6 1.6 copy-start
  14.9 7.4 copy-start.9
  14.9 7.4 copy-start.10
  14.9 185.9 %all-to-all-start.1 = ((bf16[32,20,5120]{2,1,0:T(8,128)(2,1)}), bf16[32,20,5120]{2,1,0:T(8,128)(2,1)}, u32[]{:S(2)}, u32[]{:S(2)}) async-start(bf16[32,20,5120]{2,1,0:T(8,128)(2,1)} %all_to_all.18), calls=%async_computation.1 | async-start | bytes 15728640 | tf_op jit(solution)/shard_map/all_to_all | solution.py:70
  200.8 413.7 %all-to-all-start = ((bf16[32,20,5120]{2,1,0:T(8,128)(2,1)}), bf16[32,20,5120]{2,1,0:T(8,128)(2,1)}, u32[]{:S(2)}, u32[]{:S(2)}) async-start(bf16[32,20,5120]{2,1,0:T(8,128)(2,1)} %all_to_all.16), calls=%async_computation | async-start | bytes 15728640 | tf_op jit(solution)/shard_map/all_to_all | solution.py:71
  214.5 626.3 %collective-permute-start = (bf16[3,352,5120]{2,1,0:T(8,128)(2,1)}, bf16[3,352,5120]{2,1,0:T(8,128)(2,1)}, u32[]{:S(2)}, u32[]{:S(2)}) collective-permute-start(bf16[3,352,5120]{2,1,0:T(8,128)(2,1)} %pad_maximum_fusion), channel_id=1, source_target_pairs={{0,4},{1,5},{2,6},{3,7},{4,0},{5,1},{6,2},{7,3},{8,12},{9,13},{10,... | collective-permute-start | bytes 32440328 | tf_op jit(solution)/shard_map/ppermute | solution.py:10
  617.9 9.9 slice-start
  620.9 6.9 copy-start.5
  620.9 6.9 slice-start.1
  843.9 3.2 copy-start.7
  865.6 3.6 copy-start.8
  865.6 3.7 copy-start.11
  865.6 3.9 copy-start.12
  865.6 6.8 slice-start.2
  868.7 3.1 copy-start.6
  869.6 4.0 slice-start.3
  873.6 2.9 copy-start.2
  873.6 3.1 copy-start.3
  873.6 4.1 copy-start.4
  882.8 550.3 %collective-permute-start.1 = (bf16[3,352,5120]{2,1,0:T(8,128)(2,1)}, bf16[3,352,5120]{2,1,0:T(8,128)(2,1)}, u32[]{:S(2)}, u32[]{:S(2)}) collective-permute-start(bf16[3,352,5120]{2,1,0:T(8,128)(2,1)} %pad_maximum_fusion.1), channel_id=1, source_target_pairs={{0,4},{1,5},{2,6},{3,7},{4,0},{5,1},{6,2},{7,3},{8,12},{9,13},{10,... | collective-permute-start | bytes 32440328 | tf_op jit(solution)/shard_map/ppermute | solution.py:10
  892.6 627.0 %all-to-all-start.2 = ((bf16[32,20,5120]{2,1,0:T(8,128)(2,1)}), bf16[32,20,5120]{2,1,0:T(8,128)(2,1)}, u32[]{:S(2)}, u32[]{:S(2)}) async-start(bf16[32,20,5120]{2,1,0:T(8,128)(2,1)} %pad_maximum_fusion.2), calls=%async_computation.2 | async-start | bytes 15728640 | tf_op jit(solution)/shard_map/all_to_all | solution.py:95
  902.2 9.4 slice-start.4
  906.9 4.7 slice-start.5
  906.9 4.7 copy-start.13
  1519.6 14.6 copy-start.1
where the time goes:
time: 1540 us; the launch traced here: 1530 us
  waiting for transfers between devices  1360 us (88%)
  matrix products  58.7 us (4%)
  local copies, waits for them, and re-layouts  54.9 us (4%)
  other arithmetic  33.1 us (2%)
  starting transfers between devices  23.2 us (2%)
    ppermute x2, waiting for transfers between devices, partner(): return lax.ppermute(value, axis, pairs)  729 us
    all_to_all x1, waiting for transfers between devices, local(): lax.all_to_all(copies_c, ('dp', 'expert'), split_axis=0, concat_axis=0, t...  395 us
    all_to_all x1, waiting for transfers between devices, local(): lax.all_to_all(copies_x, ('dp', 'expert'), split_axis=0, concat_axis=0, t...  166 us
    all_to_all x1, waiting for transfers between devices, local(): lax.all_to_all(part, ('dp', 'expert'), split_axis=0, concat_axis=0, tiled...  73.1 us
  transfers between devices with their start and end apart: 5, of which 5 were waited for; matrix products, arithmetic and copies ran while one was open for 4% of the time, Pallas kernels for 0%

commit v1 on v0

v1 whole, which is shorter than its diff:
```python
import jax
import jax.numpy as jnp
from jax import lax
from jax.sharding import PartitionSpec as P


def routing(clade, block, plan, columns, cap_home, cap_rows):
    experts = plan.shape[0]
    matches = clade[:, None] == jnp.arange(experts, dtype=jnp.int32)[None, :]
    lookup = jnp.sum(jnp.where(matches, plan[None, :], 0), axis=1)
    owner = jnp.where(block < cap_home, clade, (lookup + columns // 2) % columns)
    return jnp.where(block < cap_rows, owner * cap_rows + block, -1)


def local(tokens, cotangent, gate, clade, block, plan, w_gu, w_down):
    columns = lax.axis_size("expert")
    tok_rows = tokens.shape[0]
    cap_home = tok_rows // columns
    cap_guest = tok_rows // (4 * columns)
    cap_rows = cap_home + cap_guest
    slot_count = columns * cap_rows
    slot = routing(clade, block, plan, columns, cap_home, cap_rows)
    selector = (jnp.arange(slot_count, dtype=jnp.int32)[:, None] == slot[None, :]).astype(
        jnp.bfloat16
    )
    f32 = jnp.float32
    bf16 = jnp.bfloat16
    scaled = (gate[:, None] * cotangent.astype(f32)).astype(bf16)
    send_x = jnp.dot(selector, tokens, preferred_element_type=f32).astype(bf16)
    send_c = jnp.dot(selector, scaled, preferred_element_type=f32).astype(bf16)

    def spread(rows):
        mine = lax.all_to_all(rows, "expert", split_axis=0, concat_axis=0, tiled=True)
        return lax.all_gather(mine, "dp", axis=0, tiled=True)

    rows_x = spread(send_x)
    rows_c = spread(send_c)
    contract_last = (((1,), (1,)), ((), ()))
    contract_rows = (((0,), (0,)), ((), ()))
    gate_w, up_w = w_gu[0, 0], w_gu[0, 1]
    down_w = w_down[0]
    gate_pre = lax.dot_general(rows_x, gate_w, contract_last, preferred_element_type=f32)
    up_pre = lax.dot_general(rows_x, up_w, contract_last, preferred_element_type=f32)
    hidden_cot = lax.dot_general(rows_c, down_w, contract_last, preferred_element_type=f32)
    sigmoid = jax.nn.sigmoid(gate_pre)
    hidden = (gate_pre * sigmoid * up_pre).astype(bf16)
    up_cot = (hidden_cot * gate_pre * sigmoid).astype(bf16)
    gate_cot = (hidden_cot * up_pre * sigmoid * (1.0 + gate_pre * (1.0 - sigmoid))).astype(bf16)
    part = jnp.dot(gate_cot, gate_w, preferred_element_type=f32)
    part = (part + jnp.dot(up_cot, up_w, preferred_element_type=f32)).astype(bf16)
    summed = lax.psum_scatter(part, "dp", scatter_dimension=0, tiled=True)
    result = lax.all_to_all(summed, "expert", split_axis=0, concat_axis=0, tiled=True)
    d_gate = lax.dot_general(gate_cot, rows_x, contract_rows, preferred_element_type=f32)
    d_up = lax.dot_general(up_cot, rows_x, contract_rows, preferred_element_type=f32)
    d_down = lax.dot_general(hidden, rows_c, contract_rows, preferred_element_type=f32)
    grad_gu = jnp.stack([d_gate.astype(bf16), d_up.astype(bf16)])[None]
    grad_tokens = lax.dot_general(selector, result, contract_rows, preferred_element_type=f32)
    return (grad_tokens.astype(bf16), grad_gu, d_down.astype(bf16)[None])


def solution(mesh):
    placed = (
        P(("dp", "expert"), None),
        P(("dp", "expert"), None),
        P(("dp", "expert")),
        P(("dp", "expert")),
        P(("dp", "expert")),
        P(),
        P("expert", None, "dp", None),
        P("expert", "dp", None),
    )
    return jax.shard_map(
        local,
        mesh=mesh,
        in_specs=placed,
        out_specs=(
            P(("dp", "expert"), None),
            P("expert", None, "dp", None),
            P("expert", "dp", None),
        ),
        check_vma=False,
    )
```

time: 1540 us -> 316 us (0.21)
  waiting for transfers between devices: 1360 us -> 118 us
  blocking collectives: 0 us -> 102 us
  local copies, waits for them, and re-layouts: 54.9 us -> 12.4 us
  other arithmetic: 33.1 us -> 5.16 us
  starting transfers between devices: 23.2 us -> 5.82 us
    ppermute x2 -> x0, waiting for transfers between devices: 729 us -> none  [partner(): return lax.ppermute(value, axis, pairs)]
    all_to_all x3 -> x1, waiting for transfers between devices: 634 us -> 24.6 us  [local(): lax.all_to_all(summed, 'expert', split_axis=0, concat_axis=0, tiled=True)]
    all_to_all x0 -> x2, blocking collectives: none -> 102 us  [spread(): lax.all_to_all(rows, 'expert', split_axis=0, concat_axis=0, tiled=True)]
    reduce_scatter x0 -> x1, waiting for transfers between devices: none -> 60.3 us  [local(): summed = lax.psum_scatter(part, 'dp', scatter_dimension=0, tiled=True)]
    all_gather x0 -> x2, waiting for transfers between devices: none -> 33.1 us  [spread(): return lax.all_gather(mine, 'dp', axis=0, tiled=True)]
    dot_general x19 -> x11, matrix products: 58.7 us -> 58.6 us  [the longest x1 8.93 us: local(): jnp.dot(up_cot, up_w, preferred_element_type=f32)]
  transfers between devices with their start and end apart: 5 -> 4, of which waited for: 5 -> 3; matrix products, arithmetic and copies ran while one was open for 4% -> 11% of each run, Pallas kernels for 0% -> 0%
where the time goes in v1:
time: 316 us
  waiting for transfers between devices  118 us (37%)
  blocking collectives  102 us (32%)
  matrix products  58.6 us (19%)
  between operations  14 us (4%)
  local copies, waits for them, and re-layouts  12.4 us (4%)
  starting transfers between devices  5.82 us (2%)
  other arithmetic  5.16 us (2%)
    all_to_all x2, blocking collectives, spread(): lax.all_to_all(rows, 'expert', split_axis=0, concat_axis=0, tiled=True)  102 us
    reduce_scatter x1, waiting for transfers between devices, local(): summed = lax.psum_scatter(part, 'dp', scatter_dimension=0, tiled=True)  60.3 us
    all_gather x2, waiting for transfers between devices, spread(): return lax.all_gather(mine, 'dp', axis=0, tiled=True)  33.1 us
    all_to_all x1, waiting for transfers between devices, local(): lax.all_to_all(summed, 'expert', split_axis=0, concat_axis=0, tiled=True)  24.6 us
    dot_general x1, matrix products, local(): jnp.dot(up_cot, up_w, preferred_element_type=f32)  8.93 us
    all_to_all x4, local copies, waits for them, and re-layouts, spread(): lax.all_to_all(rows, 'expert', split_axis=0, concat_axis=0, tiled=True)  8.39 us
    dot_general x1, matrix products, local(): lax.dot_general(rows_c, down_w, contract_last, preferred_element_type=f32)  7.03 us
    dot_general x1, matrix products, local(): lax.dot_general(rows_x, gate_w, contract_last, preferred_element_type=f32)  7.03 us
  transfers between devices with their start and end apart: 4, of which 3 were waited for; matrix products, arithmetic and copies ran while one was open for 11% of the time, Pallas kernels for 0%

profile of v1, /device:TPU:0, one launch (start us, length us, event | category | flops | bytes accessed | tf_op | source)
XLA Modules:
  0.0 315.7 jit_solution(6076827937094635519)
XLA Ops:
  7.2 0.0 all-gather.5.cloned.1.call-start
  7.2 0.8 select_reduce_fusion
  8.1 0.7 compare_select_fusion.3
  8.8 1.8 convolution_convert_fusion.3
  10.5 1.6 all_to_all.27
  12.1 53.0 %all_to_all.36 = bf16[8,20,5120]{2,1,0:T(8,128)(2,1)} all-to-all(bf16[8,20,5120]{2,1,0:T(8,128)(2,1)S(1)} %all_to_all.27), channel_id=1, replica_groups=mesh['dp'=4,'expert'=8] {'expert'}, dimensions={0} | all-to-all | bytes 3276800 | tf_op jit(solution)/shard_map/all_to_all | solution.py:33
  65.1 2.7 all_to_all.29
  67.8 0.0 all-gather.5.cloned.1.call-update
  67.8 0.0 all-gather.3.cloned.1.call-start
  67.9 1.8 convolution_convert_fusion.4
  69.7 1.6 all_to_all.24
  71.3 48.7 %all_to_all.37 = bf16[8,20,5120]{2,1,0:T(8,128)(2,1)} all-to-all(bf16[8,20,5120]{2,1,0:T(8,128)(2,1)S(1)} %all_to_all.24), channel_id=1, replica_groups=mesh['dp'=4,'expert'=8] {'expert'}, dimensions={0} | all-to-all | bytes 3276800 | tf_op jit(solution)/shard_map/all_to_all | solution.py:33
  120.0 2.6 all_to_all.26
  122.6 0.0 all-gather.3.cloned.1.call-update
  122.6 0.2 reduce-scatter.2.cloned.1.call-start
  122.8 0.0 all-gather.5.cloned.1.call-done
  122.9 7.0 %fusion.5 = f32[640,352]{0,1:T(8,128)S(1)} fusion(bf16[640,5120]{1,0:T(8,128)(2,1)} %all-gather.5.cloned.1.call-done, bf16[1,2,352,5120]{3,2,1,0:T(8,128)(2,1)} %param.14), kind=kOutput, calls=%fused_computation.13 | convolution fusion | flops 2306867200 | bytes 11059200 | tf_op jit(solution)/shard_map/dot_general | solution.py:42
  129.9 6.3 %fusion.8 = f32[640,352]{0,1:T(8,128)S(1)} fusion(bf16[640,5120]{1,0:T(8,128)(2,1)S(1)} %copy-done.4, bf16[1,2,352,5120]{3,2,1,0:T(8,128)(2,1)} %param.14), kind=kOutput, calls=%fused_computation.16 | convolution fusion | flops 2306867200 | bytes 11059200 | tf_op jit(solution)/shard_map/dot_general | solution.py:43
  136.2 33.1 %all-gather.3.cloned.1.call-done = bf16[640,5120]{1,0:T(8,128)(2,1)} async-done(((bf16[160,5120]{1,0:T(8,128)(2,1)}), bf16[640,5120]{1,0:T(8,128)(2,1)}) %all-gather.3.cloned.1.call-update) | async-done | bytes 6553616 | tf_op jit(solution)/shard_map/all_gather | solution.py:34
  169.3 7.0 %multiply_convert_fusion.3 = (bf16[640,352]{0,1:T(8,128)(2,1)S(1)}, bf16[640,352]{0,1:T(8,128)(2,1)S(1)}) fusion(f32[640,352]{0,1:T(8,128)S(1)} %fusion.5, f32[640,352]{0,1:T(8,128)S(1)} %fusion.8, bf16[640,5120]{1,0:T(8,128)(2,1)} %all-gather.3.cloned.1.call-done, bf16[1,352,5120]{2,1,0:T(8,128)(2,1)} %param.15), kind=kOutput, calls=%fused_computation.27 | convolution fusion | flops 2309795840 | bytes 12861440 | tf_op jit(solution)/shard_map/dot_general | solution.py:44
  176.3 5.6 %fusion.3 = f32[640,5120]{1,0:T(8,128)S(1)} fusion(bf16[640,352]{0,1:T(8,128)(2,1)S(1)} %get-tuple-element.4, bf16[1,2,352,5120]{3,2,1,0:T(8,128)(2,1)} %param.14), kind=kOutput, calls=%fused_computation.11 | convolution fusion | flops 2306867200 | bytes 17162240 | tf_op jit(solution)/shard_map/dot_general | solution.py:49
  182.0 8.9 %add_convert_fusion = bf16[640,5120]{1,0:T(8,128)(2,1)} fusion(f32[640,5120]{1,0:T(8,128)S(1)} %fusion.3, bf16[640,352]{0,1:T(8,128)(2,1)S(1)} %get-tuple-element.3, bf16[1,2,352,5120]{3,2,1,0:T(8,128)(2,1)} %param.14), kind=kOutput, calls=%fused_computation | convolution fusion | flops 2313420800 | bytes 23715840 | tf_op jit(solution)/shard_map/dot_general | solution.py:50
  190.9 60.3 %reduce-scatter.2.cloned.1.call-done = bf16[160,5120]{1,0:T(8,128)(2,1)} async-done(((bf16[640,5120]{1,0:T(8,128)(2,1)}), bf16[160,5120]{1,0:T(8,128)(2,1)}) %reduce-scatter.2.cloned.1.call-update) | async-done | bytes 1638416 | tf_op jit(solution)/shard_map/reduce_scatter | solution.py:51
  251.2 2.6 all_to_all.30
  253.8 5.5 %all-to-all-start.2 = ((bf16[8,20,5120]{2,1,0:T(8,128)(2,1)}), bf16[8,20,5120]{2,1,0:T(8,128)(2,1)S(1)}, u32[]{:S(2)}, u32[]{:S(2)}) async-start(bf16[8,20,5120]{2,1,0:T(8,128)(2,1)} %all_to_all.30), calls=%async_computation.3 | async-start | bytes 3932160 | tf_op jit(solution)/shard_map/all_to_all | solution.py:52
  259.3 6.3 %fusion.1 = bf16[1,352,5120]{2,1,0:T(8,128)(2,1)S(1)} fusion(bf16[640,352]{0,1:T(8,128)(2,1)S(1)} %get-tuple-element.3, bf16[640,5120]{1,0:T(8,128)(2,1)} %all-gather.5.cloned.1.call-done), kind=kOutput, calls=%fused_computation.6 | convolution fusion | flops 2308669440 | bytes 10608640 | tf_op jit(solution)/shard_map/dot_general | solution.py:54
  265.6 6.3 %fusion = bf16[1,352,5120]{2,1,0:T(8,128)(2,1)S(1)} fusion(bf16[640,352]{0,1:T(8,128)(2,1)S(1)} %get-tuple-element.4, bf16[640,5120]{1,0:T(8,128)(2,1)} %all-gather.5.cloned.1.call-done), kind=kOutput, calls=%fused_computation.5 | convolution fusion | flops 2308669440 | bytes 10608640 | tf_op jit(solution)/shard_map/dot_general | solution.py:53
  272.1 4.5 %fusion.2 = bf16[1,352,5120]{2,1,0:T(8,128)(2,1)} fusion(bf16[640,5120]{1,0:T(8,128)(2,1)S(1)} %bitcast.36, f32[640,352]{0,1:T(8,128)S(1)} %copy-done.8, f32[640,352]{0,1:T(8,128)S(1)} %copy-done.6), kind=kOutput, calls=%fused_computation.7 | convolution fusion | flops 2310021120 | bytes 11960320 | tf_op jit(solution)/shard_map/dot_general | solution.py:55
  276.5 3.6 %maximum_bitcast_fusion = bf16[1,2,352,5120]{3,2,1,0:T(8,128)(2,1)} fusion(bf16[1,352,5120]{2,1,0:T(8,128)(2,1)S(1)} %fusion.1, bf16[1,352,5120]{2,1,0:T(8,128)(2,1)S(1)} %fusion), kind=kLoop, calls=%fused_computation.1 | loop fusion | flops 3604480 | bytes 14417920 | tf_op jit(solution)/shard_map/broadcast_in_dim | solution.py:56
  280.2 24.6 %all-to-all-done.2 = bf16[8,20,5120]{2,1,0:T(8,128)(2,1)S(1)} async-done(((bf16[8,20,5120]{2,1,0:T(8,128)(2,1)}), bf16[8,20,5120]{2,1,0:T(8,128)(2,1)S(1)}, u32[]{:S(2)}, u32[]{:S(2)}) %all-to-all-start.2) | async-done | bytes 1638432 | tf_op jit(solution)/shard_map/all_to_all | solution.py:52
  304.7 1.4 all_to_all.32
  306.1 3.0 convolution_convert_fusion.5
  (24 shorter events, 0.1 us)
Async XLA Ops:
  7.2 1.6 copy-start
  7.2 115.7 %all-gather.5.cloned.1.call-start = ((), (), s32[]{:S(2)}) async-start(), calls=%async_computation.5 | async-start | bytes 8192000 | tf_op jit(solution)/shard_map/all_gather | solution.py:34
  65.1 2.7 copy-start.2
  65.1 2.8 copy-start.3
  67.8 101.5 %all-gather.3.cloned.1.call-start = ((), (), s32[]{:S(2)}) async-start(), calls=%async_computation.4 | async-start | bytes 8192000 | tf_op jit(solution)/shard_map/all_gather | solution.py:34
  122.6 128.6 %reduce-scatter.2.cloned.1.call-start = ((), (), s32[]{:S(2)}) async-start(), calls=%async_computation.6 | async-start | bytes 8192000 | tf_op jit(solution)/shard_map/reduce_scatter | solution.py:51
  122.9 7.0 %copy-start.4 = (bf16[640,5120]{1,0:T(8,128)(2,1)S(1)}, bf16[640,5120]{1,0:T(8,128)(2,1)}, u32[]{:S(2)}) copy-start(bf16[640,5120]{1,0:T(8,128)(2,1)} %all-gather.5.cloned.1.call-done) | copy-start | bytes 19660804
  129.9 39.4 %copy-start.5 = (f32[640,352]{0,1:T(8,128)}, f32[640,352]{0,1:T(8,128)S(1)}, u32[]{:S(2)}) copy-start(f32[640,352]{0,1:T(8,128)S(1)} %fusion.5) | copy-start | bytes 2703364
  136.2 40.1 %copy-start.7 = (f32[640,352]{0,1:T(8,128)}, f32[640,352]{0,1:T(8,128)S(1)}, u32[]{:S(2)}) copy-start(f32[640,352]{0,1:T(8,128)S(1)} %fusion.8) | copy-start | bytes 2703364
  253.8 50.9 %all-to-all-start.2 = ((bf16[8,20,5120]{2,1,0:T(8,128)(2,1)}), bf16[8,20,5120]{2,1,0:T(8,128)(2,1)S(1)}, u32[]{:S(2)}, u32[]{:S(2)}) async-start(bf16[8,20,5120]{2,1,0:T(8,128)(2,1)} %all_to_all.30), calls=%async_computation.3 | async-start | bytes 3932160 | tf_op jit(solution)/shard_map/all_to_all | solution.py:52
  259.3 12.7 %slice-start = ((s8[6553600]{0:T(1024)(128)(4,1)}), s8[4194304]{0:T(1024)(128)(4,1)S(1)}, s32[]{:S(2)}) async-start(s8[6553600]{0:T(1024)(128)(4,1)} %bitcast.35), calls=%async_computation.7 | async-start | bytes 8388608
  265.6 6.4 %slice-start.1 = ((s8[6553600]{0:T(1024)(128)(4,1)}), s8[2359296]{0:T(1024)(128)(4,1)S(1)}, s32[]{:S(2)}) async-start(s8[6553600]{0:T(1024)(128)(4,1)} %bitcast.35), calls=%async_computation.8 | async-start | bytes 4718592
  265.6 6.4 %copy-start.6 = (f32[640,352]{0,1:T(8,128)S(1)}, f32[640,352]{0,1:T(8,128)}, u32[]{:S(2)}) copy-start(f32[640,352]{0,1:T(8,128)} %copy-done.5) | copy-start | bytes 2703364
  265.6 6.4 %copy-start.8 = (f32[640,352]{0,1:T(8,128)S(1)}, f32[640,352]{0,1:T(8,128)}, u32[]{:S(2)}) copy-start(f32[640,352]{0,1:T(8,128)} %copy-done.7) | copy-start | bytes 2703364
  276.5 32.6 %copy-start.1 = (bf16[128,5120]{1,0:T(8,128)(2,1)S(1)}, bf16[128,5120]{1,0:T(8,128)(2,1)}, u32[]{:S(2)}) copy-start(bf16[128,5120]{1,0:T(8,128)(2,1)} %param.8) | copy-start | bytes 3932164
Sparse Core Ops, SparseCore 0:
  67.9 46.5 all-gather.4
  122.7 46.5 all-gather.2
  191.1 60.1 reduce-scatter.1

commit v2 on v1

v2 whole, which is shorter than its diff:
```python
import functools

import jax
import jax.numpy as jnp
from jax import lax
from jax.experimental import pallas as pl
from jax.experimental.pallas import tpu as pltpu
from jax.sharding import PartitionSpec as P

F32 = jnp.float32
BF16 = jnp.bfloat16
MESH = pl.DeviceIdType.MESH
LAST = (((1,), (1,)), ((), ()))
ROWS = (((0,), (0,)), ((), ()))


def one_hot(count, index):
    return (jnp.arange(count, dtype=jnp.int32)[:, None] == index[None, :]).astype(BF16)


def place(clade, block, plan, columns, cap_home):
    experts = plan.shape[0]
    matches = clade[:, None] == jnp.arange(experts, dtype=jnp.int32)[None, :]
    lookup = jnp.sum(jnp.where(matches, plan[None, :], 0), axis=1)
    return jnp.where(block < cap_home, clade, (lookup + columns // 2) % columns)


def visit_order(columns):
    half = columns // 2
    offsets = [half]
    for step in range(1, half):
        offsets += [step, half - step, columns - step, half + step]
    seen = []
    for offset in offsets:
        if offset not in seen:
            seen.append(offset)
    return [0] + seen


def peers(columns, groups):
    d = lax.axis_index("dp")
    e = lax.axis_index("expert")
    core = d + 1 - 2 * lax.rem(d, 2)
    across = lax.rem(d + 2, groups)
    return d, e, core, across, core + 2 - 4 * (core // 2)


def greet(d, e, core, across, columns):
    barrier = pltpu.get_barrier_semaphore()
    for j in range(1, columns):
        pl.semaphore_signal(
            barrier, inc=1, device_id=(d, lax.rem(e + j, columns)), device_id_type=MESH
        )
    pl.semaphore_signal(barrier, inc=1, device_id=(core, e), device_id_type=MESH)
    pl.semaphore_signal(barrier, inc=1, device_id=(across, e), device_id_type=MESH)
    pl.semaphore_wait(barrier, columns + 1)


def dispatch_kernel(columns, groups, *refs):
    sources = refs[:3]
    outs = refs[3:6]
    local_sem, send_a, send_core, send_x, send_fwd, recv = refs[6:]
    d, e, core, across, diagonal = peers(columns, groups)
    greet(d, e, core, across, columns)
    order = visit_order(columns)
    kinds = range(3)

    def rows(index):
        return pl.ds(pl.multiple_of(index * 16, 16), 16)

    def remote(k, source, slot, send_sem, target):
        return pltpu.make_async_remote_copy(
            src_ref=source,
            dst_ref=outs[k].at[rows(slot)],
            send_sem=send_sem,
            recv_sem=recv.at[slot, k],
            device_id=target,
            device_id_type=MESH,
        )

    def arrived(k, slot):
        pltpu.make_async_copy(outs[k].at[rows(slot)], outs[k].at[rows(slot)], recv.at[slot, k]).wait()

    copies = []
    local = []
    mine = d * columns + e
    for k in kinds:
        own = sources[k].at[rows(e)]
        copies.append(remote(k, own, mine, send_x.at[0, k], (across, e)))
        copies[-1].start()
        target = lax.rem(e + order[1], columns)
        copies.append(remote(k, sources[k].at[rows(target)], mine, send_a.at[1, k], (d, target)))
        copies[-1].start()
        copies.append(remote(k, own, mine, send_core.at[0, k], (core, e)))
        copies[-1].start()
    for i in range(2, columns):
        target = lax.rem(e + order[i], columns)
        for k in kinds:
            copies.append(remote(k, sources[k].at[rows(target)], mine, send_a.at[i, k], (d, target)))
            copies[-1].start()
    for k in kinds:
        copy = pltpu.make_async_copy(sources[k].at[rows(e)], outs[k].at[rows(mine)], local_sem.at[k])
        copy.start()
        local.append(copy)
    for i in range(columns + 1):
        if 0 < i < columns:
            slot = d * columns + lax.rem(e + columns - order[i], columns)
            for k in kinds:
                arrived(k, slot)
                block = outs[k].at[rows(slot)]
                copies.append(remote(k, block, slot, send_x.at[i, k], (across, e)))
                copies[-1].start()
                copies.append(remote(k, block, slot, send_core.at[i, k], (core, e)))
                copies[-1].start()
        if i > 0:
            slot = across * columns + lax.rem(e + columns - order[i - 1], columns)
            for k in kinds:
                arrived(k, slot)
                block = outs[k].at[rows(slot)]
                copies.append(remote(k, block, slot, send_fwd.at[i - 1, k], (core, e)))
                copies[-1].start()
    for group in (core, diagonal):
        for i in range(columns):
            slot = group * columns + lax.rem(e + columns - order[i], columns)
            for k in kinds:
                arrived(k, slot)
    for copy in local:
        copy.wait()
    for copy in copies:
        copy.wait_send()


def dispatch(send_x, send_c, send_g, columns, groups, row_count):
    width = send_x.shape[1]
    senders = columns * groups
    sem = pltpu.SemaphoreType.DMA
    return pl.pallas_call(
        functools.partial(dispatch_kernel, columns, groups),
        out_shape=(
            jax.ShapeDtypeStruct((row_count, width), BF16),
            jax.ShapeDtypeStruct((row_count, width), BF16),
            jax.ShapeDtypeStruct((senders * 16, width // 2), BF16),
        ),
        in_specs=[pl.BlockSpec(memory_space=pl.ANY)] * 3,
        out_specs=(pl.BlockSpec(memory_space=pl.ANY),) * 3,
        scratch_shapes=[
            sem((3,)),
            sem((columns, 3)),
            sem((columns, 3)),
            sem((columns, 3)),
            sem((columns, 3)),
            sem((senders, 3)),
        ],
        compiler_params=pltpu.CompilerParams(collective_id=0, has_side_effects=True),
        name="dispatch",
    )(send_x, send_c, send_g)


def return_kernel(columns, groups, part_h, part_g, out_h, out_g, *scratch):
    pair_in = scratch[0:2]
    pair_out = scratch[2:4]
    cross_in = scratch[4:6]
    final = scratch[6:8]
    send_core, send_x, send_a, recv_core, recv_x, recv_a = scratch[8:]
    parts = (part_h, part_g)
    outs = (out_h, out_g)
    d, e, core, across, diagonal = peers(columns, groups)
    greet(d, e, core, across, columns)
    order = visit_order(columns)
    order = order[1:] + [0]
    kinds = range(2)

    def rows(index):
        return pl.ds(pl.multiple_of(index * 16, 16), 16)

    copies = []
    core_in = {}
    for i in range(columns):
        s = lax.rem(e + order[i], columns)
        for side, group in ((0, diagonal), (1, core)):
            for k in kinds:
                place_in = pair_in[k].at[rows(side * columns + s)]
                copy = pltpu.make_async_remote_copy(
                    src_ref=parts[k].at[rows(group * columns + s)],
                    dst_ref=place_in,
                    send_sem=send_core.at[side, i, k],
                    recv_sem=recv_core.at[side, i, k],
                    device_id=(core, e),
                    device_id_type=MESH,
                )
                copy.start()
                copies.append(copy)
                core_in[side, i, k] = copy

    def add(a, b):
        return (a[...].astype(F32) + b[...].astype(F32)).astype(BF16)

    cross = {}
    back = {}

    def finish(i):
        s = lax.rem(e + order[i], columns)
        for k in kinds:
            core_in[1, i, k].wait_recv()
            cross[i, k].wait_recv()
            final[k][rows(s)] = (
                parts[k][rows(d * columns + s)].astype(F32)
                + pair_in[k][rows(columns + s)].astype(F32)
                + cross_in[k][rows(s)].astype(F32)
            ).astype(BF16)
            if i == columns - 1:
                outs[k][rows(e)] = final[k][rows(s)]
            else:
                copy = pltpu.make_async_remote_copy(
                    src_ref=final[k].at[rows(s)],
                    dst_ref=outs[k].at[rows(e)],
                    send_sem=send_a.at[i, k],
                    recv_sem=recv_a.at[i, k],
                    device_id=(d, s),
                    device_id_type=MESH,
                )
                copy.start()
                copies.append(copy)
                back[i, k] = copy

    for i in range(columns):
        s = lax.rem(e + order[i], columns)
        for k in kinds:
            core_in[0, i, k].wait_recv()
            pair_out[k][rows(s)] = (
                parts[k][rows(across * columns + s)].astype(F32)
                + pair_in[k][rows(s)].astype(F32)
            ).astype(BF16)
            copy = pltpu.make_async_remote_copy(
                src_ref=pair_out[k].at[rows(s)],
                dst_ref=cross_in[k].at[rows(s)],
                send_sem=send_x.at[i, k],
                recv_sem=recv_x.at[i, k],
                device_id=(across, e),
                device_id_type=MESH,
            )
            copy.start()
            copies.append(copy)
            cross[i, k] = copy
        if i >= 2:
            finish(i - 2)
    finish(columns - 2)
    finish(columns - 1)
    for copy in back.values():
        copy.wait_recv()
    for copy in copies:
        copy.wait_send()


def give_back(part, part_g, columns, groups):
    width = part.shape[1]
    thin = part_g.shape[1]
    sem = pltpu.SemaphoreType.DMA
    vmem = pl.BlockSpec(memory_space=pltpu.VMEM)
    scratch = []
    for count in (2 * columns, columns, columns, columns):
        for wide in (width, thin):
            scratch.append(pltpu.VMEM((count * 16, wide), BF16))
    return pl.pallas_call(
        functools.partial(return_kernel, columns, groups),
        out_shape=(
            jax.ShapeDtypeStruct((columns * 16, width), BF16),
            jax.ShapeDtypeStruct((columns * 16, thin), BF16),
        ),
        in_specs=[vmem, vmem],
        out_specs=(vmem, vmem),
        scratch_shapes=scratch
        + [
            sem((2, columns, 2)),
            sem((columns, 2)),
            sem((columns, 2)),
            sem((2, columns, 2)),
            sem((columns, 2)),
            sem((columns, 2)),
        ],
        compiler_params=pltpu.CompilerParams(
            collective_id=1, has_side_effects=True, vmem_limit_bytes=48 * 2**20
        ),
        name="give_back",
    )(part, part_g)


def expert_pass(rows_x, rows_c, w_gu, w_down, send_part):
    gate_w, up_w, down_w = w_gu[0, 0], w_gu[0, 1], w_down[0]
    gate_pre = lax.dot_general(rows_x, gate_w, LAST, preferred_element_type=F32)
    up_pre = lax.dot_general(rows_x, up_w, LAST, preferred_element_type=F32)
    hidden_cot = lax.dot_general(rows_c, down_w, LAST, preferred_element_type=F32)
    sigmoid = jax.nn.sigmoid(gate_pre)
    hidden = (gate_pre * sigmoid * up_pre).astype(BF16)
    up_cot = (hidden_cot * gate_pre * sigmoid).astype(BF16)
    gate_cot = (hidden_cot * up_pre * sigmoid * (1.0 + gate_pre * (1.0 - sigmoid))).astype(BF16)
    part = jnp.dot(gate_cot, gate_w, preferred_element_type=F32)
    part = (part + jnp.dot(up_cot, up_w, preferred_element_type=F32)).astype(BF16)
    result = send_part(part)
    d_gate = lax.dot_general(gate_cot, rows_x, ROWS, preferred_element_type=F32)
    d_up = lax.dot_general(up_cot, rows_x, ROWS, preferred_element_type=F32)
    d_down = lax.dot_general(hidden, rows_c, ROWS, preferred_element_type=F32)
    grad_gu = jnp.stack([d_gate.astype(BF16), d_up.astype(BF16)])[None]
    return result, grad_gu, d_down.astype(BF16)[None]


def pick(selector, rows):
    return jnp.dot(selector, rows, preferred_element_type=F32).astype(BF16)


def local_general(tokens, cotangent, gate, clade, block, plan, w_gu, w_down):
    columns = lax.axis_size("expert")
    cap_home = tokens.shape[0] // columns
    cap_rows = cap_home + tokens.shape[0] // (4 * columns)
    owner = place(clade, block, plan, columns, cap_home)
    slot = jnp.where(block < cap_rows, owner * cap_rows + block, -1)
    selector = one_hot(columns * cap_rows, slot)
    scaled = (gate[:, None] * cotangent.astype(F32)).astype(BF16)

    def spread(rows):
        mine = lax.all_to_all(rows, "expert", split_axis=0, concat_axis=0, tiled=True)
        return lax.all_gather(mine, "dp", axis=0, tiled=True)

    def send_part(part):
        summed = lax.psum_scatter(part, "dp", scatter_dimension=0, tiled=True)
        return lax.all_to_all(summed, "expert", split_axis=0, concat_axis=0, tiled=True)

    rows_x = spread(pick(selector, tokens))
    rows_c = spread(pick(selector, scaled))
    result, grad_gu, grad_down = expert_pass(rows_x, rows_c, w_gu, w_down, send_part)
    grad_tokens = lax.dot_general(selector, result, ROWS, preferred_element_type=F32)
    return grad_tokens.astype(BF16), grad_gu, grad_down


def local(tokens, cotangent, gate, clade, block, plan, w_gu, w_down):
    columns = lax.axis_size("expert")
    groups = lax.axis_size("dp")
    width = tokens.shape[1]
    cap_home = tokens.shape[0] // columns
    cap_guest = tokens.shape[0] // (4 * columns)
    senders = columns * groups
    owner = place(clade, block, plan, columns, cap_home)
    is_home = block < cap_home
    is_guest = (block >= cap_home) & (block < cap_home + cap_guest)
    sel_home = one_hot(columns * cap_home, jnp.where(is_home, owner * cap_home + block, -1))
    sel_guest = one_hot(
        columns * cap_guest, jnp.where(is_guest, owner * cap_guest + block - cap_home, -1)
    )
    scaled = (gate[:, None] * cotangent.astype(F32)).astype(BF16)
    guests = jnp.stack([pick(sel_guest, tokens), pick(sel_guest, scaled)])
    guests = guests.reshape(2, columns, cap_guest, 2, width // 2).transpose(1, 0, 3, 2, 4)
    guests = guests.reshape(columns * 4 * cap_guest, width // 2)
    home_rows = senders * cap_home
    rows_x, rows_c, got = dispatch(
        pick(sel_home, tokens),
        pick(sel_home, scaled),
        guests,
        columns,
        groups,
        home_rows + senders * cap_guest,
    )
    got = got.reshape(senders, 2, 2, cap_guest, width // 2).transpose(1, 0, 3, 2, 4)
    got = got.reshape(2, senders * cap_guest, width)
    rows_x = lax.dynamic_update_slice(rows_x, got[0], (home_rows, 0))
    rows_c = lax.dynamic_update_slice(rows_c, got[1], (home_rows, 0))

    def send_part(part):
        thin = part[home_rows:].reshape(senders, cap_guest, 4, width // 4).transpose(0, 2, 1, 3)
        return give_back(part, thin.reshape(senders * 4 * cap_guest, width // 4), columns, groups)

    (home, thin), grad_gu, grad_down = expert_pass(rows_x, rows_c, w_gu, w_down, send_part)
    thin = thin.reshape(columns, 4, cap_guest, width // 4).transpose(0, 2, 1, 3)
    thin = thin.reshape(columns * cap_guest, width)
    result = lax.dot_general(sel_home, home, ROWS, preferred_element_type=F32)
    result = result + lax.dot_general(sel_guest, thin, ROWS, preferred_element_type=F32)
    return result.astype(BF16), grad_gu, grad_down


def solution(mesh):
    placed = (
        P(("dp", "expert"), None),
        P(("dp", "expert"), None),
        P(("dp", "expert")),
        P(("dp", "expert")),
        P(("dp", "expert")),
        P(),
        P("expert", None, "dp", None),
        P("expert", "dp", None),
    )

    def run(*arrays):
        columns = mesh.shape["expert"]
        each = arrays[0].shape[0] // mesh.size
        whole_blocks = each == 16 * columns and mesh.shape["dp"] == 4
        return jax.shard_map(
            local if whole_blocks else local_general,
            mesh=mesh,
            in_specs=placed,
            out_specs=(
                P(("dp", "expert"), None),
                P("expert", None, "dp", None),
                P("expert", "dp", None),
            ),
            check_vma=False,
        )(*arrays)

    return run
```

time: 316 us -> 231 us (0.73)
  Pallas kernels: 0 us -> 163 us
  waiting for transfers between devices: 118 us -> 0 us
  blocking collectives: 102 us -> 0 us
  matrix products: 58.6 us -> 41.9 us
  between operations: 14 us -> 0.93 us
  starting transfers between devices: 5.82 us -> 0 us
  local copies, waits for them, and re-layouts: 12.4 us -> 17.7 us
    pallas_call x0 -> x2, Pallas kernels: none -> 163 us  [the longest x1 104 us: dispatch(): pl.pallas_call(functools.partial(dispatch_kernel, columns, groups), out_s...]
    all_to_all x2 -> x0, blocking collectives: 102 us -> none  [spread(): lax.all_to_all(rows, 'expert', split_axis=0, concat_axis=0, tiled=True)]
    reduce_scatter x1 -> x0, waiting for transfers between devices: 60.3 us -> none  [local(): summed = lax.psum_scatter(part, 'dp', scatter_dimension=0, tiled=True)]
    all_gather x2 -> x0, waiting for transfers between devices: 33.1 us -> none  [spread(): return lax.all_gather(mine, 'dp', axis=0, tiled=True)]
    all_to_all x1 -> x0, waiting for transfers between devices: 24.6 us -> none  [local(): lax.all_to_all(summed, 'expert', split_axis=0, concat_axis=0, tiled=True)]
    dot_general x11 -> x14, matrix products: 58.6 us -> 41.9 us  [the longest x1 8.62 us: expert_pass(): jnp.dot(up_cot, up_w, preferred_element_type=F32)]
    all_to_all x6 -> x0, local copies, waits for them, and re-layouts: 12.3 us -> none  [the longest x4 8.39 us: spread(): lax.all_to_all(rows, 'expert', split_axis=0, concat_axis=0, tiled=True)]
    reshape x0 -> x7, local copies, waits for them, and re-layouts: none -> 7.85 us  [the longest x1 4.53 us: local(): got.reshape(senders, 2, 2, cap_guest, width // 2).transpose(1, 0, 3, 2, 4)]
  transfers between devices with their start and end apart: 4 -> 0, of which waited for: 3 -> 0; matrix products, arithmetic and copies ran while one was open for 11% -> 0% of each run, Pallas kernels for 0% -> 0%
where the time goes in v2:
time: 231 us
  Pallas kernels  163 us (71%)
  matrix products  41.9 us (18%)
  local copies, waits for them, and re-layouts  17.7 us (8%)
  other arithmetic  7.23 us (3%)
    pallas_call x1, Pallas kernels, dispatch(): pl.pallas_call(functools.partial(dispatch_kernel, columns, groups), out_s...  104 us
    pallas_call x1, Pallas kernels, give_back(): pl.pallas_call(functools.partial(return_kernel, columns, groups), out_sha...  59.1 us
    dot_general x1, matrix products, expert_pass(): jnp.dot(up_cot, up_w, preferred_element_type=F32)  8.62 us
    dot_general x1, matrix products, expert_pass(): part = jnp.dot(gate_cot, gate_w, preferred_element_type=F32)  5.64 us
    dot_general x4, matrix products, pick(): return jnp.dot(selector, rows, preferred_element_type=F32).astype(BF16)  5.21 us
    dot_general x1, matrix products, expert_pass(): d_down = lax.dot_general(hidden, rows_c, ROWS, preferred_element_type=F32)  4.67 us

profile of v2, /device:TPU:0, one launch (start us, length us, event | category | flops | bytes accessed | tf_op | source)
XLA Modules:
  0.0 230.8 jit_solution(12640732720910510434)
XLA Ops:
  0.6 0.9 select_reduce_fusion
  1.5 0.7 and_select_fusion
  2.2 0.7 compare_select_fusion.2
  2.9 1.7 convolution_convert_fusion.5
  4.8 0.9 copy.23
  6.4 1.4 maximum_bitcast_fusion.1
  7.8 1.0 reshape.39.refs_2_
  8.8 1.6 convolution_convert_fusion.3.refs_1_
  10.4 1.5 convolution_convert_fusion.4.refs_0_
  12.0 103.9 %dispatch.1 = (bf16[640,5120]{1,0:T(8,128)(2,1)}, bf16[640,5120]{1,0:T(8,128)(2,1)}, bf16[512,2560]{1,0:T(8,128)(2,1)}) custom-call(bf16[128,5120]{1,0:T(8,128)(2,1)} %convolution_convert_fusion.4.refs_0_, bf16[128,5120]{1,0:T(8,128)(2,1)} %convolution_convert_fusion.3.refs_1_, bf16[128,2560]{1,0:T(8,128)(2,1)} %reshape.39.refs_2_), custom_call_target="tpu_custom_call" | custom-call | tf_op jit(solution)/shard_map/dispatch/pallas_call | solution.py:137
  115.9 4.5 %reshape.40 = bf16[32,2,2,4,2560]{4,3,2,1,0:T(4,128)(2,1)S(1)} reshape(bf16[512,2560]{1,0:T(8,128)(2,1)} %get-tuple-element.9) | data formatting | bytes 5242880 | tf_op jit(solution)/shard_map/reshape | solution.py:362
  120.4 0.9 fusion.27
  121.3 1.0 copy.24
  122.6 1.0 copy.25
  123.8 1.6 copy-done.4
  125.6 1.0 slice-done
  126.6 0.9 slice-done.1
  127.5 3.0 %fusion.6 = f32[640,352]{0,1:T(8,128)S(1)} fusion(bf16[640,5120]{1,0:T(8,128)(2,1)S(1)} %get-tuple-element.19, bf16[1,2,352,5120]{3,2,1,0:T(8,128)(2,1)S(1)} %bitcast.55), kind=kOutput, calls=%fused_computation.16 | convolution fusion | flops 2306867200 | bytes 11059200 | tf_op jit(solution)/shard_map/dot_general | solution.py:290
  130.5 3.0 %fusion.9 = f32[640,352]{0,1:T(8,128)S(1)} fusion(bf16[640,5120]{1,0:T(8,128)(2,1)S(1)} %get-tuple-element.19, bf16[1,2,352,5120]{3,2,1,0:T(8,128)(2,1)S(1)} %bitcast.55), kind=kOutput, calls=%fused_computation.19 | convolution fusion | flops 2306867200 | bytes 11059200 | tf_op jit(solution)/shard_map/dot_general | solution.py:291
  133.5 3.2 %multiply_convert_fusion.2 = (bf16[640,352]{0,1:T(8,128)(2,1)S(1)}, bf16[640,352]{0,1:T(8,128)(2,1)S(1)}) fusion(f32[640,352]{0,1:T(8,128)S(1)} %fusion.6, f32[640,352]{0,1:T(8,128)S(1)} %fusion.9, bf16[640,5120]{1,0:T(8,128)(2,1)S(1)} %get-tuple-element.20, bf16[1,352,5120]{2,1,0:T(8,128)(2,1)S(1)} %copy-done.6), kind=kOutput, calls=%fused_computation.30 | convolution fusion | flops 2309795840 | bytes 12861440 | tf_op jit(solution)/shard_map/dot_general | solution.py:292
  136.7 4.7 %fusion.2 = bf16[1,352,5120]{2,1,0:T(8,128)(2,1)} fusion(bf16[640,5120]{1,0:T(8,128)(2,1)S(1)} %get-tuple-element.20, f32[640,352]{0,1:T(8,128)S(1)} %fusion.9, f32[640,352]{0,1:T(8,128)S(1)} %fusion.6), kind=kOutput, calls=%fused_computation.7 | convolution fusion | flops 2310021120 | bytes 11960320 | tf_op jit(solution)/shard_map/dot_general | solution.py:302
  141.3 3.2 %fusion.1 = bf16[1,352,5120]{2,1,0:T(8,128)(2,1)S(1)} fusion(bf16[640,352]{0,1:T(8,128)(2,1)S(1)} %get-tuple-element.17, bf16[640,5120]{1,0:T(8,128)(2,1)S(1)} %get-tuple-element.19), kind=kOutput, calls=%fused_computation.6 | convolution fusion | flops 2308669440 | bytes 10608640 | tf_op jit(solution)/shard_map/dot_general | solution.py:301
  144.5 3.2 %fusion = bf16[1,352,5120]{2,1,0:T(8,128)(2,1)S(1)} fusion(bf16[640,352]{0,1:T(8,128)(2,1)S(1)} %get-tuple-element.18, bf16[640,5120]{1,0:T(8,128)(2,1)S(1)} %get-tuple-element.19), kind=kOutput, calls=%fused_computation.5 | convolution fusion | flops 2308669440 | bytes 10608640 | tf_op jit(solution)/shard_map/dot_general | solution.py:300
  147.7 3.6 %maximum_bitcast_fusion = bf16[1,2,352,5120]{3,2,1,0:T(8,128)(2,1)} fusion(bf16[1,352,5120]{2,1,0:T(8,128)(2,1)S(1)} %fusion.1, bf16[1,352,5120]{2,1,0:T(8,128)(2,1)S(1)} %fusion), kind=kLoop, calls=%fused_computation.1 | loop fusion | flops 3604480 | bytes 14417920 | tf_op jit(solution)/shard_map/broadcast_in_dim | solution.py:303
  151.4 5.6 %fusion.4 = f32[640,5120]{1,0:T(8,128)S(1)} fusion(bf16[640,352]{0,1:T(8,128)(2,1)S(1)} %get-tuple-element.18, bf16[1,2,352,5120]{3,2,1,0:T(8,128)(2,1)} %param.14), kind=kOutput, calls=%fused_computation.14 | convolution fusion | flops 2306867200 | bytes 17162240 | tf_op jit(solution)/shard_map/dot_general | solution.py:297
  157.0 8.6 %add_convert_fusion.part_h = bf16[640,5120]{1,0:T(8,128)(2,1)} fusion(f32[640,5120]{1,0:T(8,128)S(1)} %fusion.4, bf16[640,352]{0,1:T(8,128)(2,1)S(1)} %get-tuple-element.17, bf16[1,2,352,5120]{3,2,1,0:T(8,128)(2,1)} %param.14), kind=kOutput, calls=%fused_computation | convolution fusion | flops 2313420800 | bytes 23715840 | tf_op jit(solution)/shard_map/dot_general | solution.py:298
  165.6 1.4 slice.24
  167.0 1.0 reshape.41
  168.6 0.6 reshape.42.part_g
  169.2 59.1 %give_back.1 = (bf16[128,5120]{1,0:T(8,128)(2,1)S(1)}, bf16[128,1280]{1,0:T(8,128)(2,1)S(1)}) custom-call(bf16[640,5120]{1,0:T(8,128)(2,1)} %add_convert_fusion.part_h, bf16[512,1280]{1,0:T(8,128)(2,1)S(1)} %reshape.42.part_g), custom_call_target="tpu_custom_call" | custom-call | tf_op jit(solution)/shard_map/give_back/pallas_call | solution.py:264
  228.6 0.5 fusion.21
  229.1 1.6 fusion.3
  (27 shorter events, 2.2 us)
Async XLA Ops:
  0.6 5.1 %copy-start = (bf16[128,5120]{1,0:T(8,128)(2,1)S(1)}, bf16[128,5120]{1,0:T(8,128)(2,1)}, u32[]{:S(2)}) copy-start(bf16[128,5120]{1,0:T(8,128)(2,1)} %param.8) | copy-start | bytes 3932164
  4.6 4.2 %copy-start.2 = (bf16[128,5120]{1,0:T(8,128)(2,1)S(1)}, bf16[128,5120]{1,0:T(8,128)(2,1)}, u32[]{:S(2)}) copy-start(bf16[128,5120]{1,0:T(8,128)(2,1)} %param.9) | copy-start | bytes 3932164
  4.6 4.2 %copy-start.3 = (f32[128]{0:T(128)S(1)}, f32[128]{0:T(128)}, u32[]{:S(2)}) copy-start(f32[128]{0:T(128)} %param.10) | copy-start | bytes 1540
  120.4 3.4 %copy-start.5 = (bf16[640,5120]{1,0:T(8,128)(2,1)S(1)}, bf16[640,5120]{1,0:T(8,128)(2,1)}, u32[]{:S(2)}) copy-start(bf16[640,5120]{1,0:T(8,128)(2,1)} %get-tuple-element.8) | copy-start | bytes 19660804
  121.3 4.1 %copy-start.4 = (bf16[640,5120]{1,0:T(8,128)(2,1)S(1)}, bf16[640,5120]{1,0:T(8,128)(2,1)}, u32[]{:S(2)}) copy-start(bf16[640,5120]{1,0:T(8,128)(2,1)} %get-tuple-element.10) | copy-start | bytes 19660804
  122.4 4.2 %slice-start = ((s8[7208960]{0:T(1024)(128)(4,1)}), s8[4194304]{0:T(1024)(128)(4,1)S(1)}, s32[]{:S(2)}) async-start(s8[7208960]{0:T(1024)(128)(4,1)} %bitcast.54), calls=%async_computation | async-start | bytes 8388608
  123.6 3.9 %slice-start.1 = ((s8[7208960]{0:T(1024)(128)(4,1)}), s8[3014656]{0:T(1024)(128)(4,1)S(1)}, s32[]{:S(2)}) async-start(s8[7208960]{0:T(1024)(128)(4,1)} %bitcast.54), calls=%async_computation.1 | async-start | bytes 6029312
  130.5 3.0 %copy-start.6 = (bf16[1,352,5120]{2,1,0:T(8,128)(2,1)S(1)}, bf16[1,352,5120]{2,1,0:T(8,128)(2,1)}, u32[]{:S(2)}) copy-start(bf16[1,352,5120]{2,1,0:T(8,128)(2,1)} %param.15) | copy-start | bytes 10813444
  228.6 2.2 copy-start.1

commit v3 on v2

--- a/solution.py
+++ b/solution.py
@@ -25,16 +25,13 @@
     return jnp.where(block < cap_home, clade, (lookup + columns // 2) % columns)
 
 
-def visit_order(columns):
-    half = columns // 2
-    offsets = [half]
-    for step in range(1, half):
-        offsets += [step, half - step, columns - step, half + step]
-    seen = []
-    for offset in offsets:
-        if offset not in seen:
-            seen.append(offset)
-    return [0] + seen
+def flipped(index, mask, columns):
+    total = 0
+    bit = 1
+    while bit < columns:
+        total = total + lax.rem(lax.div(index, bit) + (mask // bit) % 2, 2) * bit
+        bit *= 2
+    return total
 
 
 def peers(columns, groups):
@@ -47,9 +44,9 @@
 
 def greet(d, e, core, across, columns):
     barrier = pltpu.get_barrier_semaphore()
-    for j in range(1, columns):
+    for mask in range(1, columns):
         pl.semaphore_signal(
-            barrier, inc=1, device_id=(d, lax.rem(e + j, columns)), device_id_type=MESH
+            barrier, inc=1, device_id=(d, flipped(e, mask, columns)), device_id_type=MESH
         )
     pl.semaphore_signal(barrier, inc=1, device_id=(core, e), device_id_type=MESH)
     pl.semaphore_signal(barrier, inc=1, device_id=(across, e), device_id_type=MESH)
@@ -62,7 +59,10 @@
     local_sem, send_a, send_core, send_x, send_fwd, recv = refs[6:]
     d, e, core, across, diagonal = peers(columns, groups)
     greet(d, e, core, across, columns)
-    order = visit_order(columns)
+    half = columns // 2
+    near = [flipped(e, mask, columns) for mask in range(columns)]
+    sends = [mask for pair in zip(range(1, half + 1), range(half, columns)) for mask in pair]
+    sends = list(dict.fromkeys(sends))
     kinds = range(3)
 
     def rows(index):
@@ -88,23 +88,23 @@
         own = sources[k].at[rows(e)]
         copies.append(remote(k, own, mine, send_x.at[0, k], (across, e)))
         copies[-1].start()
-        target = lax.rem(e + order[1], columns)
-        copies.append(remote(k, sources[k].at[rows(target)], mine, send_a.at[1, k], (d, target)))
-        copies[-1].start()
+    for mask in sends:
+        target = near[mask]
+        for k in kinds:
+            source = sources[k].at[rows(target)]
+            copies.append(remote(k, source, mine, send_a.at[mask, k], (d, target)))
+            copies[-1].start()
+    for k in kinds:
+        own = sources[k].at[rows(e)]
         copies.append(remote(k, own, mine, send_core.at[0, k], (core, e)))
         copies[-1].start()
-    for i in range(2, columns):
-        target = lax.rem(e + order[i], columns)
-        for k in kinds:
-            copies.append(remote(k, sources[k].at[rows(target)], mine, send_a.at[i, k], (d, target)))
-            copies[-1].start()
     for k in kinds:
         copy = pltpu.make_async_copy(sources[k].at[rows(e)], outs[k].at[rows(mine)], local_sem.at[k])
         copy.start()
         local.append(copy)
-    for i in range(columns + 1):
+    for i in range(columns + 2):
         if 0 < i < columns:
-            slot = d * columns + lax.rem(e + columns - order[i], columns)
+            slot = d * columns + near[i]
             for k in kinds:
                 arrived(k, slot)
                 block = outs[k].at[rows(slot)]
@@ -112,16 +112,16 @@
                 copies[-1].start()
                 copies.append(remote(k, block, slot, send_core.at[i, k], (core, e)))
                 copies[-1].start()
-        if i > 0:
-            slot = across * columns + lax.rem(e + columns - order[i - 1], columns)
+        if i > 1:
+            slot = across * columns + near[i - 2]
             for k in kinds:
                 arrived(k, slot)
                 block = outs[k].at[rows(slot)]
-                copies.append(remote(k, block, slot, send_fwd.at[i - 1, k], (core, e)))
+                copies.append(remote(k, block, slot, send_fwd.at[i - 2, k], (core, e)))
                 copies[-1].start()
     for group in (core, diagonal):
         for i in range(columns):
-            slot = group * columns + lax.rem(e + columns - order[i], columns)
+            slot = group * columns + near[i]
             for k in kinds:
                 arrived(k, slot)
     for copy in local:
@@ -166,8 +166,9 @@
     outs = (out_h, out_g)
     d, e, core, across, diagonal = peers(columns, groups)
     greet(d, e, core, across, columns)
-    order = visit_order(columns)
-    order = order[1:] + [0]
+    half = columns // 2
+    order = list(range(half, columns)) + list(range(half - 1, -1, -1))
+    order = [flipped(e, mask, columns) for mask in order]
     kinds = range(2)
 
     def rows(index):
@@ -176,7 +177,7 @@
     copies = []
     core_in = {}
     for i in range(columns):
-        s = lax.rem(e + order[i], columns)
+        s = order[i]
         for side, group in ((0, diagonal), (1, core)):
             for k in kinds:
                 place_in = pair_in[k].at[rows(side * columns + s)]
@@ -192,14 +193,11 @@
                 copies.append(copy)
                 core_in[side, i, k] = copy
 
-    def add(a, b):
-        return (a[...].astype(F32) + b[...].astype(F32)).astype(BF16)
-
     cross = {}
     back = {}
 
     def finish(i):
-        s = lax.rem(e + order[i], columns)
+        s = order[i]
         for k in kinds:
             core_in[1, i, k].wait_recv()
             cross[i, k].wait_recv()
@@ -224,7 +222,7 @@
                 back[i, k] = copy
 
     for i in range(columns):
-        s = lax.rem(e + order[i], columns)
+        s = order[i]
         for k in kinds:
             core_in[0, i, k].wait_recv()
             pair_out[k][rows(s)] = (
@@ -286,22 +284,21 @@
 
 
 def expert_pass(rows_x, rows_c, w_gu, w_down, send_part):
-    gate_w, up_w, down_w = w_gu[0, 0], w_gu[0, 1], w_down[0]
-    gate_pre = lax.dot_general(rows_x, gate_w, LAST, preferred_element_type=F32)
-    up_pre = lax.dot_general(rows_x, up_w, LAST, preferred_element_type=F32)
-    hidden_cot = lax.dot_general(rows_c, down_w, LAST, preferred_element_type=F32)
+    units = w_gu.shape[2]
+    both_w = w_gu.reshape(2 * units, w_gu.shape[3])
+    pre = lax.dot_general(rows_x, both_w, LAST, preferred_element_type=F32)
+    gate_pre, up_pre = pre[:, :units], pre[:, units:]
+    hidden_cot = lax.dot_general(rows_c, w_down[0], LAST, preferred_element_type=F32)
     sigmoid = jax.nn.sigmoid(gate_pre)
     hidden = (gate_pre * sigmoid * up_pre).astype(BF16)
     up_cot = (hidden_cot * gate_pre * sigmoid).astype(BF16)
     gate_cot = (hidden_cot * up_pre * sigmoid * (1.0 + gate_pre * (1.0 - sigmoid))).astype(BF16)
-    part = jnp.dot(gate_cot, gate_w, preferred_element_type=F32)
-    part = (part + jnp.dot(up_cot, up_w, preferred_element_type=F32)).astype(BF16)
+    both_cot = jnp.concatenate([gate_cot, up_cot], axis=1)
+    part = jnp.dot(both_cot, both_w, preferred_element_type=F32).astype(BF16)
     result = send_part(part)
-    d_gate = lax.dot_general(gate_cot, rows_x, ROWS, preferred_element_type=F32)
-    d_up = lax.dot_general(up_cot, rows_x, ROWS, preferred_element_type=F32)
+    d_both = lax.dot_general(both_cot, rows_x, ROWS, preferred_element_type=F32)
     d_down = lax.dot_general(hidden, rows_c, ROWS, preferred_element_type=F32)
-    grad_gu = jnp.stack([d_gate.astype(BF16), d_up.astype(BF16)])[None]
-    return result, grad_gu, d_down.astype(BF16)[None]
+    return result, d_both.astype(BF16).reshape(w_gu.shape), d_down.astype(BF16)[None]
 
 
 def pick(selector, rows):

time: 231 us -> 196 us (0.85)
  Pallas kernels: 163 us -> 138 us
  matrix products: 41.9 us -> 34.3 us
  other arithmetic: 7.23 us -> 3.61 us
    pallas_call x1, Pallas kernels: 104 us -> 81.5 us  [dispatch(): pl.pallas_call(functools.partial(dispatch_kernel, columns, groups), out_s...]
    dot_general x7 -> x4, matrix products: 29.8 us -> 22.4 us  [the longest x1 7.8 us: expert_pass(): d_both = lax.dot_general(both_cot, rows_x, ROWS, preferred_element_type=F32)]
    broadcast_in_dim x1 -> x0, other arithmetic: 3.63 us -> none  [expert_pass(): grad_gu = jnp.stack([d_gate.astype(BF16), d_up.astype(BF16)])[None]]
    unnamed x21 -> x23, local copies, waits for them, and re-layouts: 3.93 us -> 6.62 us
    pallas_call x1, Pallas kernels: 59.1 us -> 56.4 us  [give_back(): pl.pallas_call(functools.partial(return_kernel, columns, groups), out_sha...]
where the time goes in v3:
time: 196 us; the launch traced here: 195 us
  Pallas kernels  138 us (70%)
  matrix products  34.3 us (17%)
  local copies, waits for them, and re-layouts  18.8 us (10%)
  other arithmetic  3.61 us (2%)
    pallas_call x1, Pallas kernels, dispatch(): pl.pallas_call(functools.partial(dispatch_kernel, columns, groups), out_s...  81.5 us
    pallas_call x1, Pallas kernels, give_back(): pl.pallas_call(functools.partial(return_kernel, columns, groups), out_sha...  56.4 us
    dot_general x1, matrix products, expert_pass(): d_both = lax.dot_general(both_cot, rows_x, ROWS, preferred_element_type=F32)  7.8 us
    unnamed x23, local copies, waits for them, and re-layouts  6.62 us
    dot_general x1, matrix products, expert_pass(): pre = lax.dot_general(rows_x, both_w, LAST, preferred_element_type=F32)  5.78 us
    dot_general x1, matrix products, expert_pass(): part = jnp.dot(both_cot, both_w, preferred_element_type=F32).astype(BF16)  5.58 us
    dot_general x4, matrix products, pick(): return jnp.dot(selector, rows, preferred_element_type=F32).astype(BF16)  5.22 us
    reshape x1, local copies, waits for them, and re-layouts, local(): got.reshape(senders, 2, 2, cap_guest, width // 2).transpose(1, 0, 3, 2, 4)  4.53 us

profile of v3, /device:TPU:0, one launch (start us, length us, event | category | flops | bytes accessed | tf_op | source)
XLA Modules:
  0.0 195.5 jit_solution(15726806264095781366)
XLA Ops:
  0.6 0.9 select_reduce_fusion
  1.5 0.7 and_select_fusion
  2.2 0.7 compare_select_fusion.2
  2.9 1.7 convolution_convert_fusion.5
  4.6 0.2 stack.10
  4.8 0.9 copy.23
  5.7 0.3 convolution_convert_fusion.6
  6.0 0.2 stack.9
  6.4 1.4 maximum_bitcast_fusion
  7.8 1.0 reshape.45.refs_2_
  8.8 1.6 convolution_convert_fusion.3.refs_1_
  10.4 1.6 convolution_convert_fusion.4.refs_0_
  11.9 81.5 %dispatch.1 = (bf16[640,5120]{1,0:T(8,128)(2,1)}, bf16[640,5120]{1,0:T(8,128)(2,1)}, bf16[512,2560]{1,0:T(8,128)(2,1)}) custom-call(bf16[128,5120]{1,0:T(8,128)(2,1)} %convolution_convert_fusion.4.refs_0_, bf16[128,5120]{1,0:T(8,128)(2,1)} %convolution_convert_fusion.3.refs_1_, bf16[128,2560]{1,0:T(8,128)(2,1)} %reshape.45.refs_2_), custom_call_target="tpu_custom_call" | custom-call | tf_op jit(solution)/shard_map/dispatch/pallas_call | solution.py:137
  93.4 4.5 %reshape.46 = bf16[32,2,2,4,2560]{4,3,2,1,0:T(4,128)(2,1)S(1)} reshape(bf16[512,2560]{1,0:T(8,128)(2,1)} %get-tuple-element.9) | data formatting | bytes 5242880 | tf_op jit(solution)/shard_map/reshape | solution.py:359
  98.0 0.9 fusion.16
  98.9 1.0 copy.25
  100.1 1.0 copy.24
  101.3 1.6 copy-done.5
  103.1 1.0 slice-done
  104.1 0.9 slice-done.1
  105.0 5.8 %fusion.17 = f32[640,704]{0,1:T(8,128)S(1)} fusion(bf16[640,5120]{1,0:T(8,128)(2,1)S(1)} %get-tuple-element.19, bf16[704,5120]{1,0:T(8,128)(2,1)S(1)} %bitcast.45), kind=kOutput, calls=%fused_computation.45 | convolution fusion | flops 4613734400 | bytes 15564800 | tf_op jit(solution)/shard_map/dot_general | solution.py:289
  110.8 3.2 %multiply_convert_fusion.3 = (bf16[640,352]{0,1:T(8,128)(2,1)S(1)}, bf16[640,352]{0,1:T(8,128)(2,1)S(1)}) fusion(f32[640,704]{0,1:T(8,128)S(1)} %fusion.17, bf16[640,5120]{1,0:T(8,128)(2,1)S(1)} %get-tuple-element.20, bf16[1,352,5120]{2,1,0:T(8,128)(2,1)S(1)} %copy-done.7), kind=kOutput, calls=%fused_computation.17 | convolution fusion | flops 2309795840 | bytes 12861440 | tf_op jit(solution)/shard_map/dot_general | solution.py:291
  114.0 4.5 %fusion = bf16[1,352,5120]{2,1,0:T(8,128)(2,1)} fusion(bf16[640,5120]{1,0:T(8,128)(2,1)S(1)} %get-tuple-element.20, f32[640,704]{0,1:T(8,128)S(1)} %fusion.17), kind=kOutput, calls=%fused_computation.3 | convolution fusion | flops 2310021120 | bytes 11960320 | tf_op jit(solution)/shard_map/dot_general | solution.py:300
  118.5 7.8 %convolution_convert_fusion = bf16[704,5120]{1,0:T(8,128)(2,1)} fusion(bf16[640,5120]{1,0:T(8,128)(2,1)S(1)} %get-tuple-element.19, bf16[640,352]{0,1:T(8,128)(2,1)S(1)} %get-tuple-element.16, bf16[640,352]{0,1:T(8,128)(2,1)S(1)} %get-tuple-element.15), kind=kOutput, calls=%fused_computation | convolution fusion | flops 4619141120 | bytes 14663680 | tf_op jit(solution)/shard_map/dot_general | solution.py:299
  126.3 5.6 %convolution_convert_fusion.1.part_h = bf16[640,5120]{1,0:T(8,128)(2,1)S(1)} fusion(bf16[704,5120]{1,0:T(8,128)(2,1)S(1)} %bitcast.46, bf16[640,352]{0,1:T(8,128)(2,1)S(1)} %get-tuple-element.16, bf16[640,352]{0,1:T(8,128)(2,1)S(1)} %get-tuple-element.15), kind=kOutput, calls=%fused_computation.1 | convolution fusion | flops 4618813440 | bytes 14663680 | tf_op jit(solution)/shard_map/dot_general | solution.py:297
  131.9 2.7 %copy-done.2 = bf16[640,5120]{1,0:T(8,128)(2,1)} copy-done((bf16[640,5120]{1,0:T(8,128)(2,1)}, bf16[640,5120]{1,0:T(8,128)(2,1)S(1)}, u32[]{:S(2)}) %copy-start.2) | copy-done | bytes 6553624
  134.7 1.0 reshape.48
  135.7 0.5 copy.32
  136.2 0.3 reshape.49.part_g
  136.6 56.4 %give_back.1 = (bf16[128,5120]{1,0:T(8,128)(2,1)S(1)}, bf16[128,1280]{1,0:T(8,128)(2,1)S(1)}) custom-call(bf16[640,5120]{1,0:T(8,128)(2,1)} %copy-done.2, bf16[512,1280]{1,0:T(8,128)(2,1)S(1)} %reshape.49.part_g), custom_call_target="tpu_custom_call" | custom-call | tf_op jit(solution)/shard_map/give_back/pallas_call | solution.py:262
  193.3 0.5 fusion.8
  193.8 1.6 fusion.1
  (25 shorter events, 1.0 us)
Async XLA Ops:
  0.6 5.0 %copy-start = (bf16[128,5120]{1,0:T(8,128)(2,1)S(1)}, bf16[128,5120]{1,0:T(8,128)(2,1)}, u32[]{:S(2)}) copy-start(bf16[128,5120]{1,0:T(8,128)(2,1)} %param.8) | copy-start | bytes 3932164
  5.7 3.1 %copy-start.3 = (bf16[128,5120]{1,0:T(8,128)(2,1)S(1)}, bf16[128,5120]{1,0:T(8,128)(2,1)}, u32[]{:S(2)}) copy-start(bf16[128,5120]{1,0:T(8,128)(2,1)} %param.9) | copy-start | bytes 3932164
  5.7 3.1 %copy-start.4 = (f32[128]{0:T(128)S(1)}, f32[128]{0:T(128)}, u32[]{:S(2)}) copy-start(f32[128]{0:T(128)} %param.10) | copy-start | bytes 1540
  97.9 3.4 %copy-start.6 = (bf16[640,5120]{1,0:T(8,128)(2,1)S(1)}, bf16[640,5120]{1,0:T(8,128)(2,1)}, u32[]{:S(2)}) copy-start(bf16[640,5120]{1,0:T(8,128)(2,1)} %get-tuple-element.8) | copy-start | bytes 19660804
  98.9 4.1 %copy-start.5 = (bf16[640,5120]{1,0:T(8,128)(2,1)S(1)}, bf16[640,5120]{1,0:T(8,128)(2,1)}, u32[]{:S(2)}) copy-start(bf16[640,5120]{1,0:T(8,128)(2,1)} %get-tuple-element.10) | copy-start | bytes 19660804
  99.9 4.2 %slice-start = ((s8[7208960]{0:T(1024)(128)(4,1)}), s8[4194304]{0:T(1024)(128)(4,1)S(1)}, s32[]{:S(2)}) async-start(s8[7208960]{0:T(1024)(128)(4,1)} %bitcast.43), calls=%async_computation | async-start | bytes 8388608
  101.1 3.9 %slice-start.1 = ((s8[7208960]{0:T(1024)(128)(4,1)}), s8[3014656]{0:T(1024)(128)(4,1)S(1)}, s32[]{:S(2)}) async-start(s8[7208960]{0:T(1024)(128)(4,1)} %bitcast.43), calls=%async_computation.1 | async-start | bytes 6029312
  105.0 5.8 %copy-start.7 = (bf16[1,352,5120]{2,1,0:T(8,128)(2,1)S(1)}, bf16[1,352,5120]{2,1,0:T(8,128)(2,1)}, u32[]{:S(2)}) copy-start(bf16[1,352,5120]{2,1,0:T(8,128)(2,1)} %param.15) | copy-start | bytes 10813444
  131.9 2.7 %copy-start.2 = (bf16[640,5120]{1,0:T(8,128)(2,1)}, bf16[640,5120]{1,0:T(8,128)(2,1)S(1)}, u32[]{:S(2)}) copy-start(bf16[640,5120]{1,0:T(8,128)(2,1)S(1)} %convolution_convert_fusion.1.part_h) | copy-start | bytes 19660804
  193.3 2.2 %copy-start.1 = (bf16[128,5120]{1,0:T(8,128)(2,1)S(1)}, bf16[128,5120]{1,0:T(8,128)(2,1)}, u32[]{:S(2)}) copy-start(bf16[128,5120]{1,0:T(8,128)(2,1)} %param.8) | copy-start | bytes 3932164

commit v4 on v3

--- a/solution.py
+++ b/solution.py
@@ -167,6 +167,7 @@
     d, e, core, across, diagonal = peers(columns, groups)
     greet(d, e, core, across, columns)
     half = columns // 2
+    ahead = half
     order = list(range(half, columns)) + list(range(half - 1, -1, -1))
     order = [flipped(e, mask, columns) for mask in order]
     kinds = range(2)
@@ -240,10 +241,10 @@
             copy.start()
             copies.append(copy)
             cross[i, k] = copy
-        if i >= 2:
-            finish(i - 2)
-    finish(columns - 2)
-    finish(columns - 1)
+        if i >= ahead:
+            finish(i - ahead)
+    for i in range(columns - ahead, columns):
+        finish(i)
     for copy in back.values():
         copy.wait_recv()
     for copy in copies:
@@ -356,10 +357,16 @@
         groups,
         home_rows + senders * cap_guest,
     )
-    got = got.reshape(senders, 2, 2, cap_guest, width // 2).transpose(1, 0, 3, 2, 4)
-    got = got.reshape(2, senders * cap_guest, width)
-    rows_x = lax.dynamic_update_slice(rows_x, got[0], (home_rows, 0))
-    rows_c = lax.dynamic_update_slice(rows_c, got[1], (home_rows, 0))
+    guest_rows = senders * cap_guest
+    index = jnp.arange(4 * guest_rows, dtype=jnp.int32)
+    piece, row = index // guest_rows, index % guest_rows
+    source = (row // cap_guest) * (4 * cap_guest) + piece * cap_guest + row % cap_guest
+    got = pick(one_hot(4 * guest_rows, source).T, got)
+    for piece, at in ((0, 0), (1, width // 2)):
+        lower = got[piece * guest_rows : (piece + 1) * guest_rows]
+        rows_x = lax.dynamic_update_slice(rows_x, lower, (home_rows, at))
+        upper = got[(piece + 2) * guest_rows : (piece + 3) * guest_rows]
+        rows_c = lax.dynamic_update_slice(rows_c, upper, (home_rows, at))
 
     def send_part(part):
         thin = part[home_rows:].reshape(senders, cap_guest, 4, width // 4).transpose(0, 2, 1, 3)

time: 196 us -> 193 us (0.985)
  local copies, waits for them, and re-layouts: 18.8 us -> 10.1 us
  matrix products: 34.3 us -> 40.2 us
    reshape x1 -> x0, local copies, waits for them, and re-layouts: 4.53 us -> none  [local(): got.reshape(senders, 2, 2, cap_guest, width // 2).transpose(1, 0, 3, 2, 4)]
    unnamed x23, local copies, waits for them, and re-layouts: 6.62 us -> 2.79 us
    dot_general x4 -> x5, matrix products: 5.22 us -> 8.68 us  [pick(): return jnp.dot(selector, rows, preferred_element_type=F32).astype(BF16)]
    slice x3 -> x0, local copies, waits for them, and re-layouts: 2.93 us -> none  [the longest x2 1.91 us: local(): rows_x = lax.dynamic_update_slice(rows_x, got[0], (home_rows, 0))]
    dot_general x1, matrix products: 5.78 us -> 8.29 us  [expert_pass(): pre = lax.dot_general(rows_x, both_w, LAST, preferred_element_type=F32)]
    dynamic_update_slice x1 -> x2, local copies, waits for them, and re-layouts: 0.17 us -> 2.45 us  [local(): rows_x = lax.dynamic_update_slice(rows_x, lower, (home_rows, at))]
where the time goes in v4:
time: 193 us
  Pallas kernels  138 us (72%)
  matrix products  40.2 us (21%)
  local copies, waits for them, and re-layouts  10.1 us (5%)
  other arithmetic  3.62 us (2%)
    pallas_call x1, Pallas kernels, dispatch(): pl.pallas_call(functools.partial(dispatch_kernel, columns, groups), out_s...  81.5 us
    pallas_call x1, Pallas kernels, give_back(): pl.pallas_call(functools.partial(return_kernel, columns, groups), out_sha...  56.5 us
    dot_general x5, matrix products, pick(): return jnp.dot(selector, rows, preferred_element_type=F32).astype(BF16)  8.68 us
    dot_general x1, matrix products, expert_pass(): pre = lax.dot_general(rows_x, both_w, LAST, preferred_element_type=F32)  8.29 us
    dot_general x1, matrix products, expert_pass(): d_both = lax.dot_general(both_cot, rows_x, ROWS, preferred_element_type=F32)  7.82 us
    dot_general x1, matrix products, expert_pass(): part = jnp.dot(both_cot, both_w, preferred_element_type=F32).astype(BF16)  5.58 us
    dot_general x1, matrix products, expert_pass(): d_down = lax.dot_general(hidden, rows_c, ROWS, preferred_element_type=F32)  4.44 us

profile of v4, /device:TPU:0, one launch (start us, length us, event | category | flops | bytes accessed | tf_op | source)
XLA Modules:
  0.0 192.6 jit_solution(3139234357871046003)
XLA Ops:
  0.6 0.9 select_reduce_fusion
  1.5 0.7 and_select_fusion
  2.2 0.7 compare_select_fusion.2
  2.9 1.7 convolution_convert_fusion.5
  4.6 0.2 stack.10
  4.8 0.9 copy.19
  5.7 0.3 convolution_convert_fusion.6
  6.0 0.2 stack.9
  6.2 0.1 copy.18
  6.4 1.4 maximum_bitcast_fusion
  7.8 1.0 reshape.87.refs_2_
  8.8 1.6 convolution_convert_fusion.3.refs_1_
  10.4 1.6 convolution_convert_fusion.4.refs_0_
  12.0 81.5 %dispatch.1 = (bf16[640,5120]{1,0:T(8,128)(2,1)}, bf16[640,5120]{1,0:T(8,128)(2,1)}, bf16[512,2560]{1,0:T(8,128)(2,1)}) custom-call(bf16[128,5120]{1,0:T(8,128)(2,1)} %convolution_convert_fusion.4.refs_0_, bf16[128,5120]{1,0:T(8,128)(2,1)} %convolution_convert_fusion.3.refs_1_, bf16[128,2560]{1,0:T(8,128)(2,1)} %reshape.87.refs_2_), custom_call_target="tpu_custom_call" | custom-call | tf_op jit(solution)/shard_map/dispatch/pallas_call | solution.py:137
  93.4 3.5 %convolution_convert_fusion.7 = bf16[512,2560]{1,0:T(8,128)(2,1)S(1)} fusion(bf16[512,2560]{1,0:T(8,128)(2,1)} %get-tuple-element.9, s32[512]{0:T(512)S(1)} %fusion.19), kind=kOutput, calls=%fused_computation.10 | convolution fusion | flops 1343750144 | bytes 5244928 | tf_op jit(solution)/shard_map/dot_general | solution.py:306
  96.9 1.2 slice_dynamic-update-slice_fusion.1
  98.1 1.2 slice_dynamic-update-slice_fusion
  99.4 8.3 %fusion.30 = f32[640,704]{0,1:T(8,128)S(1)} fusion(bf16[640,5120]{1,0:T(8,128)(2,1)} %get-tuple-element.17, bf16[704,5120]{1,0:T(8,128)(2,1)S(1)} %bitcast.34), kind=kOutput, calls=%fused_computation.72 | convolution fusion | flops 4613734400 | bytes 15564800 | tf_op jit(solution)/shard_map/dot_general | solution.py:290
  107.7 3.2 %multiply_convert_fusion.3 = (bf16[640,352]{0,1:T(8,128)(2,1)S(1)}, bf16[640,352]{0,1:T(8,128)(2,1)S(1)}) fusion(f32[640,704]{0,1:T(8,128)S(1)} %fusion.30, bf16[640,5120]{1,0:T(8,128)(2,1)S(1)} %copy-done.5, bf16[1,352,5120]{2,1,0:T(8,128)(2,1)S(1)} %copy-done.6), kind=kOutput, calls=%fused_computation.19 | convolution fusion | flops 2309795840 | bytes 12861440 | tf_op jit(solution)/shard_map/dot_general | solution.py:292
  110.9 4.4 %fusion = bf16[1,352,5120]{2,1,0:T(8,128)(2,1)} fusion(bf16[640,5120]{1,0:T(8,128)(2,1)S(1)} %copy-done.5, f32[640,704]{0,1:T(8,128)S(1)} %fusion.30), kind=kOutput, calls=%fused_computation.3 | convolution fusion | flops 2310021120 | bytes 11960320 | tf_op jit(solution)/shard_map/dot_general | solution.py:301
  115.4 7.8 %convolution_convert_fusion = bf16[704,5120]{1,0:T(8,128)(2,1)} fusion(bf16[640,5120]{1,0:T(8,128)(2,1)S(1)} %bitcast.37, bf16[640,352]{0,1:T(8,128)(2,1)S(1)} %get-tuple-element.16, bf16[640,352]{0,1:T(8,128)(2,1)S(1)} %get-tuple-element.15), kind=kOutput, calls=%fused_computation | convolution fusion | flops 4619141120 | bytes 14663680 | tf_op jit(solution)/shard_map/dot_general | solution.py:300
  123.2 5.6 %convolution_convert_fusion.1.part_h = bf16[640,5120]{1,0:T(8,128)(2,1)S(1)} fusion(bf16[704,5120]{1,0:T(8,128)(2,1)S(1)} %bitcast.35, bf16[640,352]{0,1:T(8,128)(2,1)S(1)} %get-tuple-element.16, bf16[640,352]{0,1:T(8,128)(2,1)S(1)} %get-tuple-element.15), kind=kOutput, calls=%fused_computation.1 | convolution fusion | flops 4618813440 | bytes 14663680 | tf_op jit(solution)/shard_map/dot_general | solution.py:298
  128.8 2.7 %copy-done.2 = bf16[640,5120]{1,0:T(8,128)(2,1)} copy-done((bf16[640,5120]{1,0:T(8,128)(2,1)}, bf16[640,5120]{1,0:T(8,128)(2,1)S(1)}, u32[]{:S(2)}) %copy-start.2) | copy-done | bytes 6553624
  131.5 0.1 slice.34
  131.6 1.0 reshape.89
  132.6 0.5 copy.24
  133.1 0.6 reshape.90.part_g
  133.7 56.5 %give_back.1 = (bf16[128,5120]{1,0:T(8,128)(2,1)S(1)}, bf16[128,1280]{1,0:T(8,128)(2,1)S(1)}) custom-call(bf16[640,5120]{1,0:T(8,128)(2,1)} %copy-done.2, bf16[512,1280]{1,0:T(8,128)(2,1)S(1)} %reshape.90.part_g), custom_call_target="tpu_custom_call" | custom-call | tf_op jit(solution)/shard_map/give_back/pallas_call | solution.py:263
  190.1 0.1 reshape.91
  190.2 0.1 copy.21
  190.4 0.5 fusion.9
  191.0 1.6 fusion.1
  (25 shorter events, 0.1 us)
Async XLA Ops:
  0.6 5.1 %copy-start = (bf16[128,5120]{1,0:T(8,128)(2,1)S(1)}, bf16[128,5120]{1,0:T(8,128)(2,1)}, u32[]{:S(2)}) copy-start(bf16[128,5120]{1,0:T(8,128)(2,1)} %param.8) | copy-start | bytes 3932164
  5.7 3.1 %copy-start.3 = (bf16[128,5120]{1,0:T(8,128)(2,1)S(1)}, bf16[128,5120]{1,0:T(8,128)(2,1)}, u32[]{:S(2)}) copy-start(bf16[128,5120]{1,0:T(8,128)(2,1)} %param.9) | copy-start | bytes 3932164
  5.7 3.1 %copy-start.4 = (f32[128]{0:T(128)S(1)}, f32[128]{0:T(128)}, u32[]{:S(2)}) copy-start(f32[128]{0:T(128)} %param.10) | copy-start | bytes 1540
  12.0 87.4 %slice-start = ((s8[7208960]{0:T(1024)(128)(4,1)}), s8[3014656]{0:T(1024)(128)(4,1)S(1)}, s32[]{:S(2)}) async-start(s8[7208960]{0:T(1024)(128)(4,1)} %bitcast.32), calls=%async_computation | async-start | bytes 6029312
  93.4 5.9 %slice-start.1 = ((s8[7208960]{0:T(1024)(128)(4,1)}), s8[4194304]{0:T(1024)(128)(4,1)S(1)}, s32[]{:S(2)}) async-start(s8[7208960]{0:T(1024)(128)(4,1)} %bitcast.32), calls=%async_computation.1 | async-start | bytes 8388608
  99.4 8.3 %copy-start.5 = (bf16[640,5120]{1,0:T(8,128)(2,1)S(1)}, bf16[640,5120]{1,0:T(8,128)(2,1)}, u32[]{:S(2)}) copy-start(bf16[640,5120]{1,0:T(8,128)(2,1)} %get-tuple-element.18) | copy-start | bytes 19660804
  99.4 8.3 %copy-start.6 = (bf16[1,352,5120]{2,1,0:T(8,128)(2,1)S(1)}, bf16[1,352,5120]{2,1,0:T(8,128)(2,1)}, u32[]{:S(2)}) copy-start(bf16[1,352,5120]{2,1,0:T(8,128)(2,1)} %param.15) | copy-start | bytes 10813444
  99.4 16.0 %slice-start.2 = ((s8[6553600]{0:T(1024)(128)(4,1)}), s8[4194304]{0:T(1024)(128)(4,1)S(1)}, s32[]{:S(2)}) async-start(s8[6553600]{0:T(1024)(128)(4,1)} %bitcast.36), calls=%async_computation.2 | async-start | bytes 8388608
  107.7 7.6 %slice-start.3 = ((s8[6553600]{0:T(1024)(128)(4,1)}), s8[2359296]{0:T(1024)(128)(4,1)S(1)}, s32[]{:S(2)}) async-start(s8[6553600]{0:T(1024)(128)(4,1)} %bitcast.36), calls=%async_computation.3 | async-start | bytes 4718592
  128.8 2.7 %copy-start.2 = (bf16[640,5120]{1,0:T(8,128)(2,1)}, bf16[640,5120]{1,0:T(8,128)(2,1)S(1)}, u32[]{:S(2)}) copy-start(bf16[640,5120]{1,0:T(8,128)(2,1)S(1)} %convolution_convert_fusion.1.part_h) | copy-start | bytes 19660804
  190.4 2.2 %copy-start.1 = (bf16[128,5120]{1,0:T(8,128)(2,1)S(1)}, bf16[128,5120]{1,0:T(8,128)(2,1)}, u32[]{:S(2)}) copy-start(bf16[128,5120]{1,0:T(8,128)(2,1)} %param.8) | copy-start | bytes 3932164

commit v5 on v4

--- a/solution.py
+++ b/solution.py
@@ -177,9 +177,10 @@
 
     copies = []
     core_in = {}
-    for i in range(columns):
-        s = order[i]
-        for side, group in ((0, diagonal), (1, core)):
+
+    def to_core(side, group):
+        for i in range(columns):
+            s = order[i]
             for k in kinds:
                 place_in = pair_in[k].at[rows(side * columns + s)]
                 copy = pltpu.make_async_remote_copy(
@@ -194,6 +195,7 @@
                 copies.append(copy)
                 core_in[side, i, k] = copy
 
+    to_core(0, diagonal)
     cross = {}
     back = {}
 
@@ -241,6 +243,8 @@
             copy.start()
             copies.append(copy)
             cross[i, k] = copy
+        if i == 0:
+            to_core(1, core)
         if i >= ahead:
             finish(i - ahead)
     for i in range(columns - ahead, columns):

time: 193 us -> 193 us (level)
  no operation moved by 1% of the time
where the time goes in v5:
time: 193 us
  Pallas kernels  138 us (72%)
  matrix products  40.2 us (21%)
  local copies, waits for them, and re-layouts  10.1 us (5%)
  other arithmetic  3.62 us (2%)
    pallas_call x1, Pallas kernels, dispatch(): pl.pallas_call(functools.partial(dispatch_kernel, columns, groups), out_s...  81.5 us
    pallas_call x1, Pallas kernels, give_back(): pl.pallas_call(functools.partial(return_kernel, columns, groups), out_sha...  56.5 us
    dot_general x5, matrix products, pick(): return jnp.dot(selector, rows, preferred_element_type=F32).astype(BF16)  8.68 us
    dot_general x1, matrix products, expert_pass(): pre = lax.dot_general(rows_x, both_w, LAST, preferred_element_type=F32)  8.29 us
    dot_general x1, matrix products, expert_pass(): d_both = lax.dot_general(both_cot, rows_x, ROWS, preferred_element_type=F32)  7.82 us
    dot_general x1, matrix products, expert_pass(): part = jnp.dot(both_cot, both_w, preferred_element_type=F32).astype(BF16)  5.58 us
    dot_general x1, matrix products, expert_pass(): d_down = lax.dot_general(hidden, rows_c, ROWS, preferred_element_type=F32)  4.44 us

profile of v5, /device:TPU:0, one launch (start us, length us, event | category | flops | bytes accessed | tf_op | source)
XLA Modules:
  0.0 192.6 jit_solution(5064009900526244040)
XLA Ops:
  0.6 0.9 select_reduce_fusion
  1.5 0.7 and_select_fusion
  2.2 0.7 compare_select_fusion.2
  2.9 1.7 convolution_convert_fusion.5
  4.6 0.2 stack.10
  4.8 0.9 copy.19
  5.7 0.3 convolution_convert_fusion.6
  6.0 0.2 stack.9
  6.2 0.1 copy.18
  6.4 1.4 maximum_bitcast_fusion
  7.8 1.0 reshape.87.refs_2_
  8.8 1.6 convolution_convert_fusion.3.refs_1_
  10.4 1.6 convolution_convert_fusion.4.refs_0_
  12.0 81.5 %dispatch.1 = (bf16[640,5120]{1,0:T(8,128)(2,1)}, bf16[640,5120]{1,0:T(8,128)(2,1)}, bf16[512,2560]{1,0:T(8,128)(2,1)}) custom-call(bf16[128,5120]{1,0:T(8,128)(2,1)} %convolution_convert_fusion.4.refs_0_, bf16[128,5120]{1,0:T(8,128)(2,1)} %convolution_convert_fusion.3.refs_1_, bf16[128,2560]{1,0:T(8,128)(2,1)} %reshape.87.refs_2_), custom_call_target="tpu_custom_call" | custom-call | tf_op jit(solution)/shard_map/dispatch/pallas_call | solution.py:137
  93.4 3.5 %convolution_convert_fusion.7 = bf16[512,2560]{1,0:T(8,128)(2,1)S(1)} fusion(bf16[512,2560]{1,0:T(8,128)(2,1)} %get-tuple-element.9, s32[512]{0:T(512)S(1)} %fusion.19), kind=kOutput, calls=%fused_computation.10 | convolution fusion | flops 1343750144 | bytes 5244928 | tf_op jit(solution)/shard_map/dot_general | solution.py:310
  96.9 1.2 slice_dynamic-update-slice_fusion.1
  98.1 1.2 slice_dynamic-update-slice_fusion
  99.4 8.3 %fusion.30 = f32[640,704]{0,1:T(8,128)S(1)} fusion(bf16[640,5120]{1,0:T(8,128)(2,1)} %get-tuple-element.17, bf16[704,5120]{1,0:T(8,128)(2,1)S(1)} %bitcast.34), kind=kOutput, calls=%fused_computation.72 | convolution fusion | flops 4613734400 | bytes 15564800 | tf_op jit(solution)/shard_map/dot_general | solution.py:294
  107.7 3.2 %multiply_convert_fusion.3 = (bf16[640,352]{0,1:T(8,128)(2,1)S(1)}, bf16[640,352]{0,1:T(8,128)(2,1)S(1)}) fusion(f32[640,704]{0,1:T(8,128)S(1)} %fusion.30, bf16[640,5120]{1,0:T(8,128)(2,1)S(1)} %copy-done.5, bf16[1,352,5120]{2,1,0:T(8,128)(2,1)S(1)} %copy-done.6), kind=kOutput, calls=%fused_computation.19 | convolution fusion | flops 2309795840 | bytes 12861440 | tf_op jit(solution)/shard_map/dot_general | solution.py:296
  110.9 4.4 %fusion = bf16[1,352,5120]{2,1,0:T(8,128)(2,1)} fusion(bf16[640,5120]{1,0:T(8,128)(2,1)S(1)} %copy-done.5, f32[640,704]{0,1:T(8,128)S(1)} %fusion.30), kind=kOutput, calls=%fused_computation.3 | convolution fusion | flops 2310021120 | bytes 11960320 | tf_op jit(solution)/shard_map/dot_general | solution.py:305
  115.4 7.8 %convolution_convert_fusion = bf16[704,5120]{1,0:T(8,128)(2,1)} fusion(bf16[640,5120]{1,0:T(8,128)(2,1)S(1)} %bitcast.37, bf16[640,352]{0,1:T(8,128)(2,1)S(1)} %get-tuple-element.16, bf16[640,352]{0,1:T(8,128)(2,1)S(1)} %get-tuple-element.15), kind=kOutput, calls=%fused_computation | convolution fusion | flops 4619141120 | bytes 14663680 | tf_op jit(solution)/shard_map/dot_general | solution.py:304
  123.2 5.6 %convolution_convert_fusion.1.part_h = bf16[640,5120]{1,0:T(8,128)(2,1)S(1)} fusion(bf16[704,5120]{1,0:T(8,128)(2,1)S(1)} %bitcast.35, bf16[640,352]{0,1:T(8,128)(2,1)S(1)} %get-tuple-element.16, bf16[640,352]{0,1:T(8,128)(2,1)S(1)} %get-tuple-element.15), kind=kOutput, calls=%fused_computation.1 | convolution fusion | flops 4618813440 | bytes 14663680 | tf_op jit(solution)/shard_map/dot_general | solution.py:302
  128.8 2.7 %copy-done.2 = bf16[640,5120]{1,0:T(8,128)(2,1)} copy-done((bf16[640,5120]{1,0:T(8,128)(2,1)}, bf16[640,5120]{1,0:T(8,128)(2,1)S(1)}, u32[]{:S(2)}) %copy-start.2) | copy-done | bytes 6553624
  131.5 0.1 slice.34
  131.6 1.0 reshape.89
  132.6 0.5 copy.24
  133.1 0.6 reshape.90.part_g
  133.7 56.5 %give_back.1 = (bf16[128,5120]{1,0:T(8,128)(2,1)S(1)}, bf16[128,1280]{1,0:T(8,128)(2,1)S(1)}) custom-call(bf16[640,5120]{1,0:T(8,128)(2,1)} %copy-done.2, bf16[512,1280]{1,0:T(8,128)(2,1)S(1)} %reshape.90.part_g), custom_call_target="tpu_custom_call" | custom-call | tf_op jit(solution)/shard_map/give_back/pallas_call | solution.py:267
  190.1 0.1 reshape.91
  190.2 0.1 copy.21
  190.4 0.5 fusion.9
  191.0 1.6 fusion.1
  (25 shorter events, 0.1 us)
Async XLA Ops:
  0.6 5.1 %copy-start = (bf16[128,5120]{1,0:T(8,128)(2,1)S(1)}, bf16[128,5120]{1,0:T(8,128)(2,1)}, u32[]{:S(2)}) copy-start(bf16[128,5120]{1,0:T(8,128)(2,1)} %param.8) | copy-start | bytes 3932164
  5.7 3.1 %copy-start.3 = (bf16[128,5120]{1,0:T(8,128)(2,1)S(1)}, bf16[128,5120]{1,0:T(8,128)(2,1)}, u32[]{:S(2)}) copy-start(bf16[128,5120]{1,0:T(8,128)(2,1)} %param.9) | copy-start | bytes 3932164
  5.7 3.1 %copy-start.4 = (f32[128]{0:T(128)S(1)}, f32[128]{0:T(128)}, u32[]{:S(2)}) copy-start(f32[128]{0:T(128)} %param.10) | copy-start | bytes 1540
  12.0 87.4 %slice-start = ((s8[7208960]{0:T(1024)(128)(4,1)}), s8[3014656]{0:T(1024)(128)(4,1)S(1)}, s32[]{:S(2)}) async-start(s8[7208960]{0:T(1024)(128)(4,1)} %bitcast.32), calls=%async_computation | async-start | bytes 6029312
  93.4 5.9 %slice-start.1 = ((s8[7208960]{0:T(1024)(128)(4,1)}), s8[4194304]{0:T(1024)(128)(4,1)S(1)}, s32[]{:S(2)}) async-start(s8[7208960]{0:T(1024)(128)(4,1)} %bitcast.32), calls=%async_computation.1 | async-start | bytes 8388608
  99.4 8.3 %copy-start.5 = (bf16[640,5120]{1,0:T(8,128)(2,1)S(1)}, bf16[640,5120]{1,0:T(8,128)(2,1)}, u32[]{:S(2)}) copy-start(bf16[640,5120]{1,0:T(8,128)(2,1)} %get-tuple-element.18) | copy-start | bytes 19660804
  99.4 8.3 %copy-start.6 = (bf16[1,352,5120]{2,1,0:T(8,128)(2,1)S(1)}, bf16[1,352,5120]{2,1,0:T(8,128)(2,1)}, u32[]{:S(2)}) copy-start(bf16[1,352,5120]{2,1,0:T(8,128)(2,1)} %param.15) | copy-start | bytes 10813444
  99.4 16.0 %slice-start.2 = ((s8[6553600]{0:T(1024)(128)(4,1)}), s8[4194304]{0:T(1024)(128)(4,1)S(1)}, s32[]{:S(2)}) async-start(s8[6553600]{0:T(1024)(128)(4,1)} %bitcast.36), calls=%async_computation.2 | async-start | bytes 8388608
  107.7 7.6 %slice-start.3 = ((s8[6553600]{0:T(1024)(128)(4,1)}), s8[2359296]{0:T(1024)(128)(4,1)S(1)}, s32[]{:S(2)}) async-start(s8[6553600]{0:T(1024)(128)(4,1)} %bitcast.36), calls=%async_computation.3 | async-start | bytes 4718592
  128.8 2.7 %copy-start.2 = (bf16[640,5120]{1,0:T(8,128)(2,1)}, bf16[640,5120]{1,0:T(8,128)(2,1)S(1)}, u32[]{:S(2)}) copy-start(bf16[640,5120]{1,0:T(8,128)(2,1)S(1)} %convolution_convert_fusion.1.part_h) | copy-start | bytes 19660804
  190.4 2.2 %copy-start.1 = (bf16[128,5120]{1,0:T(8,128)(2,1)S(1)}, bf16[128,5120]{1,0:T(8,128)(2,1)}, u32[]{:S(2)}) copy-start(bf16[128,5120]{1,0:T(8,128)(2,1)} %param.8) | copy-start | bytes 3932164
